TPU v7x, 512 devices: a whole 4x8x8 slice. The times are simulated.
512 devices in a mesh: inner: 16 (over x_lo, y), outer: 32 (over z, x_hi, core).
Axes of the slice: x: 4 (x_hi: 2, x_lo: 2; x = x_hi * 2 + x_lo), y: 8, z: 8, core: 2. Of those that a mesh axis runs over, the one named last changes fastest.
Arguments:
- acts: bfloat16 [32, 6144, 4096], P('outer', 'inner'), may hold values from -6 to 6
- grad_out: bfloat16 [32, 6144, 512], P('outer', 'inner'), may hold values from -0.019042969 to 0.019042969
- carried: float32 [32, 4096, 512], P('outer', 'inner'), may hold values from -3 to 3
- start_seed: int32 [], replicated, may hold values from 0 to 999
Outputs:
- update: bfloat16 [4096, 512], P(None, 'outer')
- new_carried: float32 [32, 4096, 512], P('outer', 'inner')
All inputs are finite; a program needn't handle non-finite values.
Results may differ from a plain program's by a relative error of at most 0.014.
Values may be sent and summed in bfloat16 or wider, within the bound.
No kernel may reach another device: no remote copies, remote signals or barrier semaphores. Data moves between devices by JAX's collectives and lax.ppermute only.
A program may use at most 64 MiB of HBM per device.

v0:
```python
import jax
import jax.numpy as jnp
from jax import lax
from jax.sharding import PartitionSpec as P

RANK = 64


def seeded_start(start_seed, width, rank_size):
    index = jnp.arange(width * rank_size, dtype=jnp.int32)
    seed_term = jnp.asarray(start_seed, jnp.int32) * jnp.int32(19349663)
    hashed = index * jnp.int32(73856093) ^ seed_term
    hashed = hashed ^ lax.shift_right_logical(hashed, jnp.int32(13))
    hashed = hashed * jnp.int32(1274126177)
    hashed = hashed ^ lax.shift_right_logical(hashed, jnp.int32(16))
    fraction = (hashed & jnp.int32(16777215)).astype(jnp.float32) / 16777216.0
    return (fraction - 0.5).reshape(width, rank_size)


def per_device(acts, grad_out, carried, start_seed):
    local_x = acts[0]
    local_v = grad_out[0]
    width = local_v.shape[1]
    grad = lax.psum_scatter(
        lax.dot_general(
            local_x, local_v, (((0,), (0,)), ((), ())), preferred_element_type=jnp.float32
        ).astype(jnp.bfloat16),
        "inner",
        scatter_dimension=0,
        tiled=True,
    ).astype(jnp.float32)
    work = grad + carried[0]
    start = seeded_start(start_seed, width, RANK)
    left = lax.psum(jnp.dot(work, start, precision=lax.Precision.HIGHEST), "outer")
    gram = lax.psum(jnp.dot(left.T, left, precision=lax.Precision.HIGHEST), "inner")
    chol = jnp.linalg.cholesky(gram)
    basis = lax.linalg.triangular_solve(chol, left, left_side=False, lower=True, transpose_a=True)
    right_part = jnp.dot(work.T, basis, precision=lax.Precision.HIGHEST)
    right = lax.psum(right_part, ("inner", "outer"))
    right = right / lax.axis_size("outer")
    approx = jnp.dot(basis, right.T, precision=lax.Precision.HIGHEST)
    col_count = width // lax.axis_size("outer")
    col_start = lax.axis_index("outer") * col_count
    mine = lax.dynamic_slice_in_dim(approx, col_start, col_count, 1).astype(jnp.bfloat16)
    update = lax.all_gather(mine, "inner", axis=0, tiled=True)
    return (update, (work - approx)[None])


def solution(mesh):
    placed = (P("outer", "inner", None), P("outer", "inner", None), P("outer", "inner", None), P())
    return jax.shard_map(
        per_device,
        mesh=mesh,
        in_specs=placed,
        out_specs=(P(None, "outer"), P("outer", "inner", None)),
        check_vma=False,
    )
```

profile of v0, /device:TPU:1, one launch (start us, length us, event | category | flops | bytes accessed | tf_op | source)
XLA Modules:
  0.0 731.9 jit_solution(1133016527926906654)
XLA Ops:
  7.2 0.0 copy-start
  7.2 0.0 reduce-scatter.2.cloned.1.call-start
  7.2 1.8 copy-done
  9.1 5.3 convolution_convert_fusion
  14.4 0.0 reduce-scatter.2.cloned.1.call-update
  14.4 0.0 all-reduce.3.cloned.1.call-start
  15.1 76.8 %reduce-scatter.2.cloned.1.call-done = bf16[256,512]{1,0:T(8,128)(2,1)} async-done(((bf16[4096,512]{1,0:T(8,128)(2,1)}), bf16[256,512]{1,0:T(8,128)(2,1)}) %reduce-scatter.2.cloned.1.call-update) | async-done | bytes 262160 | tf_op jit(solution)/shard_map/reduce_scatter | solution.py:24
  91.9 0.0 copy-start.2
  91.9 2.4 fusion.5
  94.3 0.0 all-reduce.3.cloned.1.call-update
  94.3 0.0 all-reduce.5.cloned.1.call-start
  94.4 248.1 %all-reduce.3.cloned.1.call-done = f32[256,64]{0,1:T(8,128)} async-done(((f32[256,64]{0,1:T(8,128)}), f32[256,64]{0,1:T(8,128)}) %all-reduce.3.cloned.1.call-update) | async-done | bytes 65552 | tf_op jit(solution)/shard_map/psum | solution.py:34
  342.5 1.1 fusion.41
  343.6 48.8 %psum.22 = f32[64,64]{0,1:T(8,128)S(1)} all-reduce(f32[64,64]{0,1:T(8,128)S(1)} %fusion.41), channel_id=1, replica_groups=mesh['inner'=16,'outer'=32] {'inner'}, use_global_device_ids=true, to_apply=%region_2.0 | all-reduce | flops 4096 | bytes 32768 | tf_op jit(solution)/shard_map/psum | solution.py:35
  392.4 0.1 copy.10
  392.5 5.8 cholesky.16
  398.4 0.6 compare_reduce_fusion
  399.0 0.7 fusion.28
  399.7 4.9 custom-call.6
  404.6 1.1 fusion.29
  405.7 2.8 fusion.4
  408.5 0.0 all-reduce.5.cloned.1.call-update
  408.5 275.6 %all-reduce.5.cloned.1.call-done = f32[512,64]{1,0:T(8,128)} async-done(((f32[512,64]{1,0:T(8,128)}), f32[512,64]{1,0:T(8,128)}) %all-reduce.5.cloned.1.call-update) | async-done | bytes 131088 | tf_op jit(solution)/shard_map/psum | solution.py:39
  684.1 1.6 fusion.2
  685.7 0.0 copy-start.1
  685.7 0.8 copy-done.1
  686.5 0.1 dynamic-slice_convert_fusion
  686.6 34.5 %all_gather.3 = bf16[4096,16]{1,0:T(8,128)(2,1)} all-gather(bf16[256,16]{1,0:T(8,128)(2,1)S(1)} %dynamic-slice_convert_fusion), channel_id=1, replica_groups=mesh['inner'=16,'outer'=32] {'inner'}, dimensions={0}, use_global_device_ids=true | all-gather | bytes 139264 | tf_op jit(solution)/shard_map/all_gather | solution.py:45
  721.1 2.2 copy.11
  723.3 0.0 copy-done.2
  723.3 2.1 subtract_bitcast_fusion
  (2 shorter events, 0.0 us)
Async XLA Ops:
  7.2 1.9 copy-start
  7.2 84.7 %reduce-scatter.2.cloned.1.call-start = ((), (), s32[]{:S(2)}) async-start(), calls=%async_computation.1 | async-start | bytes 4456448 | tf_op jit(solution)/shard_map/reduce_scatter | solution.py:24
  14.4 328.1 %all-reduce.3.cloned.1.call-start = ((), (), s32[]{:S(2)}) async-start(), calls=%async_computation.2 | async-start | bytes 131072 | tf_op jit(solution)/shard_map/psum | solution.py:34
  91.9 631.4 %copy-start.2 = (bf16[256,512]{1,0:T(8,128)(2,1)S(1)}, bf16[256,512]{1,0:T(8,128)(2,1)}, u32[]{:S(2)}) copy-start(bf16[256,512]{1,0:T(8,128)(2,1)} %reduce-scatter.2.cloned.1.call-done) | copy-start | bytes 786436
  94.3 589.7 %all-reduce.5.cloned.1.call-start = ((), (), s32[]{:S(2)}) async-start(), calls=%async_computation.3 | async-start | bytes 524288 | tf_op jit(solution)/shard_map/psum | solution.py:39
  685.7 0.8 copy-start.1
Sparse Core Ops, SparseCore 0:
  14.5 77.3 reduce-scatter.1
  95.4 247.0 all-reduce.2
  408.6 275.4 all-reduce.4
where the time goes:
time: 736 us; the launch traced here: 732 us
  waiting for transfers between devices  601 us (82%)
  blocking collectives  83.3 us (11%)
  between operations  14.5 us (2%)
  matrix products  14.3 us (2%)
  other arithmetic  14.2 us (2%)
    psum x1, waiting for transfers between devices, per_device(): right = lax.psum(right_part, ('inner', 'outer'))  276 us
    psum x1, waiting for transfers between devices, per_device(): lax.psum(jnp.dot(work, start, precision=lax.Precision.HIGHEST), 'outer')  248 us
    reduce_scatter x1, waiting for transfers between devices, per_device(): lax.psum_scatter(lax.dot_general(local_x, local_v, (((0,), (0,)), ((), ()...  76.8 us
    psum x1, blocking collectives, per_device(): lax.psum(jnp.dot(left.T, left, precision=lax.Precision.HIGHEST), 'inner')  48.8 us
    all_gather x1, blocking collectives, per_device(): update = lax.all_gather(mine, 'inner', axis=0, tiled=True)  34.5 us
  transfers between devices with their start and end apart: 3, of which 3 were waited for; matrix products, arithmetic and copies ran while one was open for 0% of the time, Pallas kernels for 0%

commit v1 on v0

v1 whole, which is shorter than its diff:
```python
import jax
import jax.numpy as jnp
from jax import lax
from jax.sharding import PartitionSpec as P

RANK = 64
HI = lax.Precision.HIGHEST
F32 = jnp.float32
BF16 = jnp.bfloat16


def seeded_start(start_seed, width, rank_size):
    index = jnp.arange(width * rank_size, dtype=jnp.int32)
    seed_term = jnp.asarray(start_seed, jnp.int32) * jnp.int32(19349663)
    hashed = index * jnp.int32(73856093) ^ seed_term
    hashed = hashed ^ lax.shift_right_logical(hashed, jnp.int32(13))
    hashed = hashed * jnp.int32(1274126177)
    hashed = hashed ^ lax.shift_right_logical(hashed, jnp.int32(16))
    fraction = (hashed & jnp.int32(16777215)).astype(jnp.float32) / 16777216.0
    return (fraction - 0.5).reshape(width, rank_size)


def split2(a, axis):
    high = a.astype(BF16)
    low = (a - high.astype(F32)).astype(BF16)
    return jnp.concatenate([high, low], axis)


def spread(piece, count):
    return jnp.broadcast_to(piece[None], (count,) + piece.shape)


def per_device(acts, grad_out, carried, start_seed):
    x, v, c = acts[0], grad_out[0], carried[0]
    tokens, feats = x.shape
    width = v.shape[1]
    rows = c.shape[0]
    n_in, n_out = lax.axis_size("inner"), lax.axis_size("outer")
    inner, outer = lax.axis_index("inner"), lax.axis_index("outer")
    core = outer % 2
    half = rows // 2
    siblings = [(i, i ^ 1) for i in range(n_out)]
    same_core = [[i for i in range(n_out) if i % 2 == k] for k in range(2)]

    partial = lax.dot_general(x, v, (((0,), (0,)), ((), ())), preferred_element_type=F32).astype(BF16)
    grad = lax.psum_scatter(partial, "inner", scatter_dimension=0, tiled=True)

    start = seeded_start(start_seed, width, RANK)
    with jax.named_scope("left_part"):
        vs = jnp.dot(v.astype(F32), start, precision=HI)
        both = lax.dot_general(split2(vs, 1), x, (((0,), (0,)), ((), ())), preferred_element_type=F32)
        left_t = both[:RANK] + both[RANK:]
        own = lax.dot_general(start, c, (((0,), (1,)), ((), ())), precision=HI)
        at = (0, inner * rows)
        left_t = lax.dynamic_update_slice(left_t, lax.dynamic_slice(left_t, at, own.shape) + own, at)
        chunks = left_t.reshape(RANK, n_in, 2, half).transpose(2, 1, 0, 3)
    with jax.named_scope("left_sum"):
        keep = lax.dynamic_index_in_dim(chunks, core, 0, False)
        give = lax.dynamic_index_in_dim(chunks, 1 - core, 0, False)
        pair = keep + lax.ppermute(give, "outer", siblings)
        got = lax.all_to_all(pair.astype(BF16), "inner", 0, 0)
        mine = jnp.sum(got.astype(F32), 0).astype(BF16)
        got = lax.all_to_all(spread(mine, n_out // 2), "outer", 0, 0, axis_index_groups=same_core)
        mine = jnp.sum(got.astype(F32), 0).astype(BF16)
    with jax.named_scope("left_gather"):
        near = lax.all_to_all(spread(mine, n_in), "inner", 0, 0)
        far = lax.ppermute(near, "outer", siblings)
        first = core == 0
        whole = jnp.stack([jnp.where(first, near, far), jnp.where(first, far, near)])
        left_t = whole.transpose(2, 1, 0, 3).reshape(RANK, feats)
        own_t = lax.dynamic_slice(left_t, at, (RANK, rows))
    with jax.named_scope("right_part"):
        y = lax.dot_general(x, left_t, (((1,), (1,)), ((), ())), preferred_element_type=F32)
        both = lax.dot_general(v, split2(y, 1), (((0,), (0,)), ((), ())), preferred_element_type=F32)
        m = both[:, :RANK] + both[:, RANK:]
        m = m + lax.dot_general(c, own_t.astype(F32), (((0,), (1,)), ((), ())), precision=HI)
        packed = jnp.concatenate([m[: width // 2], m[width // 2 :]], 1).reshape(n_out, -1, 2 * RANK)
    with jax.named_scope("right_sum"):
        mine = jnp.sum(lax.all_to_all(packed, "outer", 0, 0), 0)
        mine = jnp.sum(lax.all_to_all(spread(mine, n_in), "inner", 0, 0), 0)
        packed = lax.all_to_all(spread(mine, n_out), "outer", 0, 0).reshape(width // 2, 2 * RANK)
        m = jnp.concatenate([packed[:, :RANK], packed[:, RANK:]], 0)
    with jax.named_scope("factor"):
        gram = lax.dot_general(left_t, left_t, (((1,), (1,)), ((), ())), preferred_element_type=F32)
        chol = jnp.linalg.cholesky(gram)
        inv = lax.linalg.triangular_solve(chol, jnp.eye(RANK, dtype=F32), left_side=True, lower=True)
    with jax.named_scope("result"):
        right_t = lax.dot_general(inv, m, (((1,), (1,)), ((), ())), precision=HI) / n_out
        q = lax.dot_general(inv, right_t, (((0,), (0,)), ((), ())), precision=HI)
        cols = width // n_out
        q_mine = lax.dynamic_slice_in_dim(q, outer * cols, cols, 1)
        update = lax.dot_general(left_t.astype(F32), q_mine, (((0,), (0,)), ((), ())), precision=HI).astype(BF16)
        approx = lax.dot_general(own_t.astype(F32), q, (((0,), (0,)), ((), ())), precision=HI)
        return (update, (grad.astype(F32) + c - approx)[None])


def solution(mesh):
    placed = (P("outer", "inner", None), P("outer", "inner", None), P("outer", "inner", None), P())
    return jax.shard_map(
        per_device,
        mesh=mesh,
        in_specs=placed,
        out_specs=(P(None, "outer"), P("outer", "inner", None)),
        check_vma=False,
    )
```

time: 736 us -> 170 us (0.23)
  waiting for transfers between devices: 601 us -> 17.8 us
  starting transfers between devices: 0.12 us -> 34.8 us
  blocking collectives: 83.3 us -> 52.5 us
  local copies, waits for them, and re-layouts: 4.99 us -> 14.6 us
    psum x2 -> x0, waiting for transfers between devices: 524 us -> none  [the longest x1 276 us: per_device(): right = lax.psum(right_part, ('inner', 'outer'))]
    reduce_scatter x1, waiting for transfers between devices: 76.8 us -> 0.01 us  [per_device(): grad = lax.psum_scatter(partial, 'inner', scatter_dimension=0, tiled=True)]
    all_to_all x0 -> x3, blocking collectives: none -> 52.5 us  [the longest x1 22.8 us: per_device(): lax.all_to_all(spread(mine, n_out // 2), 'outer', 0, 0, axis_index_groups...]
    psum x1 -> x0, blocking collectives: 48.8 us -> none  [per_device(): lax.psum(jnp.dot(left.T, left, precision=lax.Precision.HIGHEST), 'inner')]
    all_gather x1 -> x0, blocking collectives: 34.5 us -> none  [per_device(): update = lax.all_gather(mine, 'inner', axis=0, tiled=True)]
    all_to_all x0 -> x3, starting transfers between devices: none -> 18.8 us  [the longest x1 8.05 us: per_device(): lax.all_to_all(spread(mine, n_out), 'outer', 0, 0)]
    ppermute x0 -> x2, starting transfers between devices: none -> 16 us  [the longest x1 8.79 us: per_device(): pair = keep + lax.ppermute(give, 'outer', siblings)]
    all_to_all x0 -> x3, waiting for transfers between devices: none -> 15 us  [the longest x1 6.73 us: per_device(): mine = jnp.sum(lax.all_to_all(spread(mine, n_in), 'inner', 0, 0), 0)]
  transfers between devices with their start and end apart: 3 -> 6, of which waited for: 3 -> 5; matrix products, arithmetic and copies ran while one was open for 0% -> 23% of each run, Pallas kernels for 0% -> 0%
where the time goes in v1:
time: 170 us; the launch traced here: 169 us
  blocking collectives  52.5 us (31%)
  starting transfers between devices  34.8 us (20%)
  matrix products  20.1 us (12%)
  waiting for transfers between devices  17.8 us (10%)
  between operations  15 us (9%)
  other arithmetic  14.7 us (9%)
  local copies, waits for them, and re-layouts  14.6 us (9%)
    all_to_all x1, blocking collectives, per_device(): lax.all_to_all(spread(mine, n_out // 2), 'outer', 0, 0, axis_index_groups...  22.8 us
    all_to_all x1, blocking collectives, per_device(): got = lax.all_to_all(pair.astype(BF16), 'inner', 0, 0)  15.5 us
    all_to_all x1, blocking collectives, per_device(): near = lax.all_to_all(spread(mine, n_in), 'inner', 0, 0)  14.1 us
    ppermute x1, starting transfers between devices, per_device(): pair = keep + lax.ppermute(give, 'outer', siblings)  8.79 us
    all_to_all x1, starting transfers between devices, per_device(): lax.all_to_all(spread(mine, n_out), 'outer', 0, 0)  8.05 us
    ppermute x1, starting transfers between devices, per_device(): far = lax.ppermute(near, 'outer', siblings)  7.23 us
    all_to_all x1, starting transfers between devices, per_device(): mine = jnp.sum(lax.all_to_all(packed, 'outer', 0, 0), 0)  7.03 us
    all_to_all x1, waiting for transfers between devices, per_device(): mine = jnp.sum(lax.all_to_all(spread(mine, n_in), 'inner', 0, 0), 0)  6.73 us
  transfers between devices with their start and end apart: 6, of which 5 were waited for; matrix products, arithmetic and copies ran while one was open for 23% of the time, Pallas kernels for 0%

profile of v1, /device:TPU:1, one launch (start us, length us, event | category | flops | bytes accessed | tf_op | source)
XLA Modules:
  0.0 169.4 jit_solution(5193194440327299736)
XLA Ops:
  7.2 0.0 copy-start
  7.2 0.0 reduce-scatter.2.cloned.1.call-start
  7.2 1.8 %copy-done = bf16[1,384,4096]{2,1,0:T(8,128)(2,1)S(1)} copy-done((bf16[1,384,4096]{2,1,0:T(8,128)(2,1)S(1)}, bf16[1,384,4096]{2,1,0:T(8,128)(2,1)}, u32[]{:S(2)}) %copy-start) | copy-done | bytes 3145752
  9.1 5.3 %convolution_convert_fusion = bf16[4096,512]{1,0:T(8,128)(2,1)} fusion(bf16[1,384,4096]{2,1,0:T(8,128)(2,1)S(1)} %copy-done, bf16[1,384,512]{2,1,0:T(8,128)(2,1)} %param.5), kind=kOutput, calls=%fused_computation | convolution fusion | flops 1612709888 | bytes 7733248 | tf_op jit(solution)/shard_map/dot_general | solution.py:45
  14.4 0.0 reduce-scatter.2.cloned.1.call-update
  15.1 0.1 fusion.25
  15.1 0.1 sub.19
  15.2 1.6 subtract_convert_fusion.1
  16.8 0.0 copy-start.1
  16.8 0.7 fusion.3
  17.5 1.1 slice_add_fusion
  18.6 0.0 copy-done.1
  18.6 2.1 %fusion.10 = f32[64,4096]{1,0:T(8,128)} fusion(f32[64,4096]{1,0:T(8,128)} %slice_add_fusion, s32[]{:T(128)S(6)} %select_n.40, f32[512,64]{1,0:T(8,128)S(1)} %sub.19, f32[1,256,512]{2,1,0:T(8,128)S(1)} %copy-done.1), kind=kOutput, calls=%fused_computation.16 | convolution fusion | flops 100679680 | bytes 786436 | tf_op jit(solution)/shard_map/left_part/dot_general | solution.py:53
  20.7 3.1 %reshape.42 = f32[64,16,2,128]{3,2,1,0:T(2,128)} reshape(f32[64,4096]{1,0:T(8,128)} %fusion.10) | data formatting | bytes 2097152 | tf_op jit(solution)/shard_map/left_part/reshape | solution.py:56
  23.8 2.7 %constant_dynamic-slice_fusion.1 = (f32[64,16,1,128]{3,2,1,0:T(1,128)S(1)}, f32[64,16,1,128]{3,2,1,0:T(1,128)S(1)}) fusion(f32[64,16,2,128]{3,2,1,0:T(2,128)} %reshape.42, s32[]{:T(128)S(6)} %select_n.41, s32[]{:T(128)S(6)} %select_n.42), kind=kLoop, calls=%fused_computation.68 | loop fusion | bytes 2097160 | tf_op jit(solution)/shard_map/dynamic-slice
  26.5 0.2 copy.35
  26.7 8.8 %collective-permute-start = (f32[16,64,128]{2,1,0:T(8,128)S(1)}, f32[16,64,128]{2,1,0:T(8,128)S(1)}, u32[]{:S(2)}, u32[]{:S(2)}) collective-permute-start(f32[16,64,128]{2,1,0:T(8,128)S(1)} %bitcast.86), channel_id=1, source_target_pairs={{0,1},{1,0},{2,3},{3,2},{4,5},{5,4},{6,7},{7,6},{8,9},{9,8},{10,11... | collective-permute-start | bytes 1572872 | tf_op jit(solution)/shard_map/left_sum/ppermute | solution.py:60
  35.5 1.5 collective-permute-done
  37.0 0.2 fusion.12
  37.2 15.5 %all_to_all.30 = bf16[16,64,128]{2,1,0:T(8,128)(2,1)S(1)} all-to-all(bf16[16,64,128]{2,1,0:T(8,128)(2,1)S(1)} %fusion.12), channel_id=1, replica_groups=mesh['inner'=16,'outer'=32] {'inner'}, dimensions={0} | all-to-all | bytes 524288 | tf_op jit(solution)/shard_map/left_sum/all_to_all | solution.py:61
  52.8 22.8 %all_to_all.31 = bf16[16,64,128]{2,1,0:T(8,128)(2,1)S(1)} all-to-all(bf16[16,64,128]{2,1,0:T(8,128)(2,1)S(1)} %broadcast_in_dim.11), channel_id=1, replica_groups={{0,2,4,6,8,10,12,14,16,18,20,22,24,26,28,30},{1,3,5,7,9,11,13,15,17,19,..., dimensions={0} | all-to-all | bytes 524288 | tf_op jit(solution)/shard_map/left_sum/all_to_all | solution.py:63
  75.8 14.1 %all_to_all.32 = bf16[16,64,128]{2,1,0:T(8,128)(2,1)S(1)} all-to-all(bf16[16,64,128]{2,1,0:T(8,128)(2,1)S(1)} %broadcast_in_dim.12), channel_id=1, replica_groups=mesh['inner'=16,'outer'=32] {'inner'}, dimensions={0} | all-to-all | bytes 524288 | tf_op jit(solution)/shard_map/left_gather/all_to_all | solution.py:66
  89.9 7.2 %collective-permute-start.1 = (bf16[16,64,128]{2,1,0:T(8,128)(2,1)S(1)}, bf16[16,64,128]{2,1,0:T(8,128)(2,1)}, u32[]{:S(2)}, u32[]{:S(2)}) collective-permute-start(bf16[16,64,128]{2,1,0:T(8,128)(2,1)S(1)} %all_to_all.32), channel_id=1, source_target_pairs={{0,1},{1,0},{2,3},{3,2},{4,5},{5,4},{6,7},{7,6},{8,9},{9,8},{10,11... | collective-permute-start | bytes 786440 | tf_op jit(solution)/shard_map/left_gather/ppermute | solution.py:67
  97.1 1.3 collective-permute-done.1
  98.4 1.0 select_bitcast_fusion.1
  99.4 0.0 copy-start.4
  99.4 0.0 copy-start.5
  99.4 0.7 copy-done.4
  100.1 0.1 copy-done.5
  100.2 0.1 maximum_bitcast_fusion
  100.3 0.0 copy-start.3
  100.3 1.3 copy.23
  101.6 2.2 %reshape.43 = bf16[64,4096]{1,0:T(8,128)(2,1)} reshape(bf16[64,16,2,128]{3,2,1,0:T(2,128)(2,1)} %copy.23) | data formatting | bytes 1048576 | tf_op jit(solution)/shard_map/left_gather/reshape | solution.py:70
  103.8 0.0 copy-start.2
  103.8 2.2 %subtract_convert_fusion = (bf16[384,64]{0,1:T(8,128)(2,1)S(1)}, bf16[384,64]{0,1:T(8,128)(2,1)S(1)}) fusion(bf16[64,4096]{1,0:T(8,128)(2,1)} %reshape.43, bf16[1,384,4096]{2,1,0:T(8,128)(2,1)S(1)} %copy-done), kind=kOutput, calls=%fused_computation.50 | convolution fusion | flops 201424896 | bytes 3768320 | tf_op jit(solution)/shard_map/right_part/dot_general | solution.py:73
  106.0 0.0 copy-done.3
  106.0 0.2 convolution_bitcast_fusion
  106.3 0.0 copy-done.2
  106.3 1.1 fusion.6
  107.4 0.8 copy.25
  108.2 7.0 %all-to-all-start.3 = ((f32[32,8,128]{2,1,0:T(8,128)}), f32[32,8,128]{2,1,0:T(8,128)S(1)}, u32[]{:S(2)}, u32[]{:S(2)}) async-start(f32[32,8,128]{2,1,0:T(8,128)} %bitcast.21), calls=%async_computation.3 | async-start | bytes 262144 | tf_op jit(solution)/shard_map/right_sum/all_to_all | solution.py:79
  115.2 1.5 convolution_bitcast_fusion.3
  116.7 0.1 copy.24
  116.8 5.8 %cholesky.17 = f32[64,64]{1,0:T(8,128)S(1)} custom-call(f32[64,64]{1,0:T(8,128)S(1)} %fusion.35), custom_call_target="Cholesky" | custom-call | tf_op jit(solution)/shard_map/factor/jit(cholesky)/cholesky | solution.py:85
  122.6 3.3 %all-to-all-done.3 = f32[32,8,128]{2,1,0:T(8,128)S(1)} async-done(((f32[32,8,128]{2,1,0:T(8,128)}), f32[32,8,128]{2,1,0:T(8,128)S(1)}, u32[]{:S(2)}, u32[]{:S(2)}) %all-to-all-start.3) | async-done | bytes 131104 | tf_op jit(solution)/shard_map/right_sum/all_to_all | solution.py:79
  126.0 0.6 broadcast_in_dim.13
  126.6 3.7 %all-to-all-start.4 = ((f32[16,8,128]{2,1,0:T(8,128)}), f32[16,8,128]{2,1,0:T(8,128)S(1)}, u32[]{:S(2)}, u32[]{:S(2)}) async-start(f32[16,8,128]{2,1,0:T(8,128)} %broadcast_in_dim.13), calls=%async_computation.4 | async-start | bytes 131072 | tf_op jit(solution)/shard_map/right_sum/all_to_all | solution.py:80
  130.4 0.6 compare_reduce_fusion
  131.0 6.7 %all-to-all-done.4 = f32[16,8,128]{2,1,0:T(8,128)S(1)} async-done(((f32[16,8,128]{2,1,0:T(8,128)}), f32[16,8,128]{2,1,0:T(8,128)S(1)}, u32[]{:S(2)}, u32[]{:S(2)}) %all-to-all-start.4) | async-done | bytes 65568 | tf_op jit(solution)/shard_map/right_sum/all_to_all | solution.py:80
  137.7 0.7 broadcast_in_dim.14
  138.4 8.0 %all-to-all-start.5 = ((f32[32,8,128]{2,1,0:T(8,128)}), f32[32,8,128]{2,1,0:T(8,128)S(1)}, u32[]{:S(2)}, u32[]{:S(2)}) async-start(f32[32,8,128]{2,1,0:T(8,128)} %broadcast_in_dim.14), calls=%async_computation.5 | async-start | bytes 262144 | tf_op jit(solution)/shard_map/right_sum/all_to_all | solution.py:81
  146.5 0.7 fusion.32
  147.1 4.9 %custom-call.6 = f32[1,64,64]{1,2,0:T(8,128)S(1)} custom-call(f32[1,64,64]{2,1,0:T(8,128)S(1)} %fusion.32), custom_call_target="InvertDiagBlocksLowerTriangular" | custom-call | tf_op jit(solution)/shard_map/factor/triangular_solve | solution.py:86
  152.0 0.2 fusion.33
  152.3 5.0 %all-to-all-done.5 = f32[32,8,128]{2,1,0:T(8,128)S(1)} async-done(((f32[32,8,128]{2,1,0:T(8,128)}), f32[32,8,128]{2,1,0:T(8,128)S(1)}, u32[]{:S(2)}, u32[]{:S(2)}) %all-to-all-start.5) | async-done | bytes 131104 | tf_op jit(solution)/shard_map/right_sum/all_to_all | solution.py:81
  157.2 0.1 fusion.45
  157.3 0.4 convolution_multiply_fusion
  157.7 0.3 fusion.47
  158.0 2.2 %convolution_convert_fusion.1 = bf16[4096,16]{0,1:T(8,128)(2,1)} fusion(bf16[64,4096]{1,0:T(8,128)(2,1)} %reshape.43, f32[64,512]{1,0:T(8,128)S(1)} %fusion.47, s32[]{:T(128)S(6)} %select_n.46), kind=kOutput, calls=%fused_computation.1 | convolution fusion | flops 50397184 | bytes 688132 | tf_op jit(solution)/shard_map/result/dot_general | solution.py:92
  160.2 0.0 reduce-scatter.2.cloned.1.call-done
  160.2 2.3 %fusion.5 = f32[1,256,512]{2,1,0:T(8,128)} fusion(f32[64,512]{1,0:T(8,128)S(1)} %fusion.47, f32[1,256,512]{2,1,0:T(8,128)} %param.6, bf16[256,512]{1,0:T(8,128)(2,1)} %reduce-scatter.2.cloned.1.call-done, bf16[64,4096]{1,0:T(8,128)(2,1)} %reshape.43, s32[]{:T(128)S(6)} %select_n.40), kind=kOutput, calls=%fused_computation.8 | convolution fusion | flops 101056512 | bytes 1474564 | tf_op jit(solution)/shard_map/result/dot_general | solution.py:93
  (10 shorter events, 0.3 us)
Async XLA Ops:
  7.2 1.9 %copy-start = (bf16[1,384,4096]{2,1,0:T(8,128)(2,1)S(1)}, bf16[1,384,4096]{2,1,0:T(8,128)(2,1)}, u32[]{:S(2)}) copy-start(bf16[1,384,4096]{2,1,0:T(8,128)(2,1)} %param.4) | copy-start | bytes 9437188
  7.2 153.0 %reduce-scatter.2.cloned.1.call-start = ((), (), s32[]{:S(2)}) async-start(), calls=%async_computation.7 | async-start | bytes 4456448 | tf_op jit(solution)/shard_map/reduce_scatter | solution.py:46
  16.8 1.8 %copy-start.1 = (f32[1,256,512]{2,1,0:T(8,128)S(1)}, f32[1,256,512]{2,1,0:T(8,128)}, u32[]{:S(2)}) copy-start(f32[1,256,512]{2,1,0:T(8,128)} %param.6) | copy-start | bytes 1572868
  26.7 10.3 %collective-permute-start = (f32[16,64,128]{2,1,0:T(8,128)S(1)}, f32[16,64,128]{2,1,0:T(8,128)S(1)}, u32[]{:S(2)}, u32[]{:S(2)}) collective-permute-start(f32[16,64,128]{2,1,0:T(8,128)S(1)} %bitcast.86), channel_id=1, source_target_pairs={{0,1},{1,0},{2,3},{3,2},{4,5},{5,4},{6,7},{7,6},{8,9},{9,8},{10,11... | collective-permute-start | bytes 1572872 | tf_op jit(solution)/shard_map/left_sum/ppermute | solution.py:60
  89.9 8.5 %collective-permute-start.1 = (bf16[16,64,128]{2,1,0:T(8,128)(2,1)S(1)}, bf16[16,64,128]{2,1,0:T(8,128)(2,1)}, u32[]{:S(2)}, u32[]{:S(2)}) collective-permute-start(bf16[16,64,128]{2,1,0:T(8,128)(2,1)S(1)} %all_to_all.32), channel_id=1, source_target_pairs={{0,1},{1,0},{2,3},{3,2},{4,5},{5,4},{6,7},{7,6},{8,9},{9,8},{10,11... | collective-permute-start | bytes 786440 | tf_op jit(solution)/shard_map/left_gather/ppermute | solution.py:67
  99.4 0.7 copy-start.4
  99.4 0.8 copy-start.5
  100.3 5.8 %copy-start.3 = (bf16[1,384,512]{2,1,0:T(8,128)(2,1)S(1)}, bf16[1,384,512]{2,1,0:T(8,128)(2,1)}, u32[]{:S(2)}) copy-start(bf16[1,384,512]{2,1,0:T(8,128)(2,1)} %param.5) | copy-start | bytes 1179652
  103.8 2.4 %copy-start.2 = (f32[1,256,512]{2,1,0:T(8,128)S(1)}, f32[1,256,512]{2,1,0:T(8,128)}, u32[]{:S(2)}) copy-start(f32[1,256,512]{2,1,0:T(8,128)} %param.6) | copy-start | bytes 1572868
  108.2 17.8 %all-to-all-start.3 = ((f32[32,8,128]{2,1,0:T(8,128)}), f32[32,8,128]{2,1,0:T(8,128)S(1)}, u32[]{:S(2)}, u32[]{:S(2)}) async-start(f32[32,8,128]{2,1,0:T(8,128)} %bitcast.21), calls=%async_computation.3 | async-start | bytes 262144 | tf_op jit(solution)/shard_map/right_sum/all_to_all | solution.py:79
  126.6 11.1 %all-to-all-start.4 = ((f32[16,8,128]{2,1,0:T(8,128)}), f32[16,8,128]{2,1,0:T(8,128)S(1)}, u32[]{:S(2)}, u32[]{:S(2)}) async-start(f32[16,8,128]{2,1,0:T(8,128)} %broadcast_in_dim.13), calls=%async_computation.4 | async-start | bytes 131072 | tf_op jit(solution)/shard_map/right_sum/all_to_all | solution.py:80
  138.4 18.8 %all-to-all-start.5 = ((f32[32,8,128]{2,1,0:T(8,128)}), f32[32,8,128]{2,1,0:T(8,128)S(1)}, u32[]{:S(2)}, u32[]{:S(2)}) async-start(f32[32,8,128]{2,1,0:T(8,128)} %broadcast_in_dim.14), calls=%async_computation.5 | async-start | bytes 262144 | tf_op jit(solution)/shard_map/right_sum/all_to_all | solution.py:81
Sparse Core Ops, SparseCore 0:
  14.5 88.2 reduce-scatter.1

commit v2 on v0

v2 whole, which is shorter than its diff:
```python
import functools

import jax
import jax.numpy as jnp
from jax import lax
from jax.experimental import pallas as pl
from jax.experimental.pallas import tpu as pltpu
from jax.sharding import PartitionSpec as P

RANK = 64
LANES = 128
HI = lax.Precision.HIGHEST
F32 = jnp.float32
BF16 = jnp.bfloat16
MIB = 1024 * 1024
CUTS = (20, 42)


def seeded_start_t(seed, width):
    shape = (RANK, width)
    index = lax.broadcasted_iota(jnp.int32, shape, 1) * RANK + lax.broadcasted_iota(jnp.int32, shape, 0)
    hashed = index * jnp.int32(73856093) ^ (seed * jnp.int32(19349663))
    hashed = hashed ^ lax.shift_right_logical(hashed, jnp.int32(13))
    hashed = hashed * jnp.int32(1274126177)
    hashed = hashed ^ lax.shift_right_logical(hashed, jnp.int32(16))
    return (hashed & jnp.int32(16777215)).astype(F32) / 16777216.0 - 0.5


def terms(a, count):
    out = []
    for _ in range(count):
        out.append(a.astype(BF16))
        a = a - out[-1].astype(F32)
    return out


def dot(a, b, dims, **kw):
    return lax.dot_general(a, b, (dims, ((), ())), preferred_element_type=F32, **kw)


NN = ((1,), (0,))
NT = ((1,), (1,))
TN = ((0,), (0,))


def position():
    outer = lax.axis_index("outer")
    return lax.axis_index("inner"), outer, lax.rem(outer, 2)


def in_hbm(a):
    return pltpu.with_memory_space_constraint(a, pltpu.HBM)


def in_vmem(a):
    return pltpu.with_memory_space_constraint(a, pltpu.VMEM)


def fetch(pairs, sems):
    copies = [pltpu.make_async_copy(a, b, sems.at[k]) for k, (a, b) in enumerate(pairs)]
    for copy in copies:
        copy.start()
    return copies


def first_kernel(seed_ref, v_hbm, c_hbm, x_hbm, keep_ref, give_ref, part_hbm, v_ref, c_ref, x_ref, part_ref, in_sems, out_sems):
    inner, _, core = position()
    count, tokens, wide = x_ref.shape
    blocks = [(x_hbm.at[:, pl.ds(j * wide, wide)], x_ref.at[j]) for j in range(count)]
    v_copy, c_copy, *x_copies = fetch([(v_hbm, v_ref), (c_hbm, c_ref)] + blocks, in_sems)
    start_t = seeded_start_t(seed_ref[0], v_ref.shape[1])
    start_3 = jnp.concatenate(terms(start_t, 3), 0)
    v_copy.wait()
    parts = dot(start_3, v_ref[...], NT)
    vs_t = parts[:RANK] + parts[RANK : 2 * RANK] + parts[2 * RANK :]
    v_t = v_ref[...].astype(F32).T.astype(BF16)
    lhs = jnp.concatenate(terms(vs_t, 2) + [v_t], 0)
    c_copy.wait()
    c_2 = terms(c_ref[...], 2)
    cs = dot(start_3, c_2[0], NT) + dot(start_3, c_2[1], NT)
    cs = cs[:RANK] + cs[RANK : 2 * RANK] + cs[2 * RANK :]
    per = wide // (2 * LANES)
    out_copies = []
    for j in range(count):
        x_copies[j].wait()
        both = dot(lhs, x_ref[j], NN)
        left = both[:RANK] + both[RANK : 2 * RANK]
        for n in range(per):
            k = j * per + n
            cols = slice(2 * n * LANES, 2 * (n + 1) * LANES)
            block = left[:, cols] + (inner == k).astype(F32) * cs
            even, odd = block[:, :LANES], block[:, LANES:]
            keep_ref[k] = jnp.where(core == 0, even, odd)
            give_ref[k] = jnp.where(core == 0, odd, even)
            part_ref[k] = both[2 * RANK :, cols].astype(BF16)
        span = pl.ds(j * per, per)
        out_copies += fetch([(part_ref.at[span], part_hbm.at[span])], out_sems.at[pl.ds(j, 1)])
    for copy in out_copies:
        copy.wait()


def first_part(seed, v, c, x, n_in):
    tokens, feats = x.shape
    width = v.shape[1]
    count = 8
    vmem, hbm = pl.BlockSpec(memory_space=pltpu.VMEM), pl.BlockSpec(memory_space=pltpu.HBM)
    out = pltpu.VMEM((n_in, RANK, LANES), F32)
    part = pltpu.HBM((n_in, width, 2 * LANES), BF16)
    return pl.pallas_call(
        first_kernel,
        in_specs=[pl.BlockSpec(memory_space=pltpu.SMEM), hbm, hbm, hbm],
        out_specs=[vmem, vmem, hbm],
        out_shape=[out, out, part],
        scratch_shapes=[
            pltpu.VMEM(v.shape, BF16),
            pltpu.VMEM(c.shape, F32),
            pltpu.VMEM((count, tokens, feats // count), BF16),
            pltpu.VMEM((n_in, width, 2 * LANES), BF16),
            pltpu.SemaphoreType.DMA((count + 2,)),
            pltpu.SemaphoreType.DMA((count,)),
        ],
        compiler_params=pltpu.CompilerParams(vmem_limit_bytes=16 * MIB),
        name="first_part",
    )(seed, in_hbm(v), in_hbm(c), in_hbm(x))


def in_order(core, near, far):
    first = core == 0
    near, far = near.astype(F32), far.astype(F32)
    return jnp.concatenate([jnp.where(first, near, far), jnp.where(first, far, near)], 1).astype(BF16)


def right_kernel(near_ref, far_ref, x_ref, v_hbm, c_hbm, out_ref, aug_ref, v_ref, c_ref, sems):
    inner, _, core = position()
    copies = fetch([(v_hbm, v_ref), (c_hbm, c_ref)], sems)
    y = gram = 0.0
    per = 2
    for k in range(0, near_ref.shape[0], per):
        left = jnp.concatenate([in_order(core, near_ref[k + n], far_ref[k + n]) for n in range(per)], 1)
        y += dot(x_ref[:, 2 * k * LANES : 2 * (k + per) * LANES], left, NT)
        gram += dot(left, left, NT)
    eye = lax.broadcasted_iota(jnp.int32, gram.shape, 0) == lax.broadcasted_iota(jnp.int32, gram.shape, 1)
    aug_ref[...] = jnp.concatenate([gram, eye.astype(F32)], 1)
    y_2 = jnp.concatenate(terms(y.T, 2), 0)
    own = in_order(core, near_ref[inner], far_ref[inner])
    for copy in copies:
        copy.wait()
    both = dot(y_2, v_ref[...], NN)
    m = both[:RANK] + both[RANK:]
    for term in terms(c_ref[...], 2):
        m += dot(own, term, NN)
    high = out_ref.shape[1]
    across = m.shape[1] // LANES
    for k in range(out_ref.shape[0]):
        r, q = divmod(k, across)
        out_ref[k] = m[high * r : high * (r + 1), q * LANES : (q + 1) * LANES].astype(out_ref.dtype)


def right_part(near, far, v, c, x):
    high = 16
    tiles = RANK // high * (v.shape[1] // LANES)
    vmem, hbm = pl.BlockSpec(memory_space=pltpu.VMEM), pl.BlockSpec(memory_space=pltpu.HBM)
    return pl.pallas_call(
        right_kernel,
        in_specs=[vmem, vmem, vmem, hbm, hbm],
        out_specs=[vmem, vmem],
        out_shape=[jax.ShapeDtypeStruct((tiles, high, LANES), BF16), pltpu.VMEM((RANK, 2 * RANK), F32)],
        scratch_shapes=[pltpu.VMEM(v.shape, BF16), pltpu.VMEM(c.shape, F32), pltpu.SemaphoreType.DMA((2,))],
        compiler_params=pltpu.CompilerParams(vmem_limit_bytes=12 * MIB),
        name="right_part",
    )(in_vmem(near), in_vmem(far), x, in_hbm(v), in_hbm(c))


def eliminate(aug, begin, end):
    blocks = [aug[8 * k : 8 * k + 8] for k in range(RANK // 8)]
    below = lax.broadcasted_iota(jnp.int32, blocks[0].shape, 0)
    for j in range(begin, end):
        at, sub = divmod(j, 8)
        row = blocks[at][sub : sub + 1]
        scaled = row / row[:, j : j + 1]
        for k in range(at, len(blocks)):
            taken = blocks[k][:, j : j + 1] * scaled
            blocks[k] = blocks[k] - (jnp.where(below > sub, taken, 0.0) if k == at else taken)
    return jnp.concatenate(blocks, 0)


def more_kernel(begin, end, aug_ref, out_ref):
    aug = eliminate(aug_ref[...], begin, end)
    if end == RANK:
        shape = (RANK, 2 * RANK)
        eye = lax.broadcasted_iota(jnp.int32, shape, 0) == lax.broadcasted_iota(jnp.int32, shape, 1)
        pivots = jnp.sum(jnp.where(eye, aug, 0.0), 1, keepdims=True)
        aug = aug * lax.rsqrt(pivots)
    out_ref[...] = aug


def more_call(begin, end, name, aug):
    vmem = pl.BlockSpec(memory_space=pltpu.VMEM)
    return pl.pallas_call(
        functools.partial(more_kernel, begin, end),
        in_specs=[vmem],
        out_specs=vmem,
        out_shape=pltpu.VMEM(aug.shape, F32),
        compiler_params=pltpu.CompilerParams(vmem_limit_bytes=4 * MIB),
        cost_estimate=pl.CostEstimate(flops=4_000_000, bytes_accessed=2_000_000, transcendentals=0),
        name=name,
    )(aug)


def result_kernel(n_out, tiles_ref, inv_ref, near_ref, far_ref, grad_hbm, c_hbm, update_hbm, new_hbm, update_ref, new_ref, grad_ref, c_ref, in_sems, out_sems):
    copies = fetch([(grad_hbm, grad_ref), (c_hbm, c_ref)], in_sems)
    inner, outer, core = position()
    high = tiles_ref.shape[1]
    across = tiles_ref.shape[0] * high // RANK
    m_t = jnp.concatenate(
        [jnp.concatenate([tiles_ref[r * across + q] for q in range(across)], 1) for r in range(RANK // high)], 0
    ).astype(F32)
    inv = inv_ref[:, RANK:]
    right_t = dot(inv, m_t, NN, precision=HI) / n_out
    q = dot(inv, right_t, TN, precision=HI)
    q_2 = terms(q, 2)
    own = in_order(core, near_ref[inner], far_ref[inner])
    approx = dot(jnp.concatenate([own, own], 0), jnp.concatenate(q_2, 0), TN)
    for copy in copies:
        copy.wait()
    new_ref[...] = grad_ref[...].astype(F32).T + c_ref[...] - approx
    rows = new_ref.shape[0] // 2
    out = [(new_ref.at[pl.ds(k * rows, rows)], new_hbm.at[pl.ds(k * rows, rows)]) for k in range(2)]
    out_copies = fetch(out, out_sems)
    cols = update_ref.shape[0]
    shape = (cols, q.shape[1])
    pick = lax.broadcasted_iota(jnp.int32, shape, 1) == outer * cols + lax.broadcasted_iota(jnp.int32, shape, 0)
    pick = pick.astype(BF16)
    q_mine = jnp.concatenate([dot(pick, term, NT).astype(BF16) for term in q_2], 0)
    for i in range(near_ref.shape[0]):
        both = dot(q_mine, in_order(core, near_ref[i], far_ref[i]), NN)
        update_ref[:, 2 * i * LANES : 2 * (i + 1) * LANES] = (both[:cols] + both[cols:]).astype(BF16)
    out_copies += fetch([(update_ref, update_hbm)], out_sems.at[pl.ds(2, 1)])
    for copy in out_copies:
        copy.wait()


def result(tiles, inv, near, far, grad_t, c, n_out):
    vmem, hbm = pl.BlockSpec(memory_space=pltpu.VMEM), pl.BlockSpec(memory_space=pltpu.HBM)
    update = jax.ShapeDtypeStruct((c.shape[1] // n_out, near.shape[0] * 2 * LANES), BF16)
    return pl.pallas_call(
        functools.partial(result_kernel, n_out),
        in_specs=[vmem] * 4 + [hbm] * 2,
        out_specs=[hbm, hbm],
        out_shape=[update, jax.ShapeDtypeStruct(c.shape, F32)],
        scratch_shapes=[
            pltpu.VMEM(update.shape, BF16),
            pltpu.VMEM(c.shape, F32),
            pltpu.VMEM(grad_t.shape, BF16),
            pltpu.VMEM(c.shape, F32),
            pltpu.SemaphoreType.DMA((2,)),
            pltpu.SemaphoreType.DMA((3,)),
        ],
        compiler_params=pltpu.CompilerParams(vmem_limit_bytes=12 * MIB),
        name="result",
    )(tiles, inv, in_vmem(near), in_vmem(far), in_hbm(grad_t), in_hbm(c))


def spread(piece, count):
    return jnp.broadcast_to(piece[None], (count,) + piece.shape)


def chip_groups(n_in, n_out):
    column, plane = {}, {}
    for i in range(n_in * n_out):
        inner, outer = divmod(i, n_out)
        z, x_hi, core = outer // 4, outer // 2 % 2, outer % 2
        column.setdefault((inner, x_hi), []).append(i)
        plane.setdefault((z, core), []).append(i)
    return list(column.values()), list(plane.values())


def per_device(acts, grad_out, carried, start_seed):
    x, v, c = acts[0], grad_out[0], carried[0]
    n_in, n_out = lax.axis_size("inner"), lax.axis_size("outer")
    siblings = [(i, i ^ 1) for i in range(n_out)]
    same_core = [[i for i in range(n_out) if i % 2 == k] for k in range(2)]

    keep, give, part = first_part(start_seed.reshape(1), v, c, x, n_in)
    with jax.named_scope("left_sum"):
        pair = (keep + lax.ppermute(give, "outer", siblings)).astype(BF16)
        got = lax.all_to_all(pair, "inner", 0, 0)
        mine = jnp.sum(got.astype(F32), 0).astype(BF16)
        part, mine = lax.optimization_barrier((part, mine))
        got = lax.all_to_all(spread(mine, n_out // 2), "outer", 0, 0, axis_index_groups=same_core)
        mine = jnp.sum(got.astype(F32), 0).astype(BF16)
    with jax.named_scope("grad"):
        grad_t = lax.psum_scatter(part.reshape(-1, part.shape[2]), "inner", scatter_dimension=0, tiled=True)
    with jax.named_scope("left_gather"):
        near = lax.all_to_all(spread(mine, n_in), "inner", 0, 0)
        far = lax.ppermute(near, "outer", siblings)
    tiles, aug = right_part(near, far, v, c, x)
    with jax.named_scope("right_sum"):
        both_axes = ("inner", "outer")
        column, plane = chip_groups(n_in, n_out)
        aug = more_call(0, CUTS[0], "factor_a", aug)
        got = lax.all_to_all(tiles, both_axes, 0, 0, axis_index_groups=column)
        mine = jnp.sum(got.astype(F32), 0).astype(BF16)
        aug, mine = lax.optimization_barrier((aug, mine))
        aug = more_call(CUTS[0], CUTS[1], "factor_b", aug)
        got = lax.all_to_all(spread(mine, len(plane[0])), both_axes, 0, 0, axis_index_groups=plane)
        mine = jnp.sum(got.astype(F32), 0).astype(BF16)
        aug, mine = lax.optimization_barrier((aug, mine))
        inv = more_call(CUTS[1], RANK, "factor_c", aug)
        tiles = lax.all_to_all(spread(mine, len(column[0])), both_axes, 0, 0, axis_index_groups=column)
    update_t, new_carried = result(tiles, inv, near, far, grad_t, c, n_out)
    return (update_t.T, new_carried[None])


def solution(mesh):
    placed = (P("outer", "inner", None), P("outer", "inner", None), P("outer", "inner", None), P())
    return jax.shard_map(
        per_device,
        mesh=mesh,
        in_specs=placed,
        out_specs=(P(None, "outer"), P("outer", "inner", None)),
        check_vma=False,
    )
```

time: 736 us -> 139 us (0.19)
  waiting for transfers between devices: 601 us -> 24.3 us
  blocking collectives: 83.3 us -> 51 us
  starting transfers between devices: 0.12 us -> 28.3 us
  Pallas kernels: 0 us -> 17.8 us
  matrix products: 14.3 us -> 0 us
  other arithmetic: 14.2 us -> 0.22 us
    psum x2 -> x0, waiting for transfers between devices: 524 us -> none  [the longest x1 276 us: per_device(): right = lax.psum(right_part, ('inner', 'outer'))]
    reduce_scatter x1, waiting for transfers between devices: 76.8 us -> 0.01 us  [per_device(): lax.psum_scatter(part.reshape(-1, part.shape[2]), 'inner', scatter_dimens...]
    all_to_all x0 -> x3, blocking collectives: none -> 51 us  [the longest x1 22.9 us: per_device(): lax.all_to_all(spread(mine, n_out // 2), 'outer', 0, 0, axis_index_groups...]
    psum x1 -> x0, blocking collectives: 48.8 us -> none  [per_device(): lax.psum(jnp.dot(left.T, left, precision=lax.Precision.HIGHEST), 'inner')]
    all_gather x1 -> x0, blocking collectives: 34.5 us -> none  [per_device(): update = lax.all_gather(mine, 'inner', axis=0, tiled=True)]
    all_to_all x0 -> x3, waiting for transfers between devices: none -> 21.6 us  [the longest x1 9.32 us: per_device(): lax.all_to_all(spread(mine, len(plane[0])), both_axes, 0, 0, axis_index_g...]
    pallas_call x0 -> x6, Pallas kernels: none -> 17.8 us  [the longest x1 6.88 us: first_part(): pl.pallas_call(first_kernel, in_specs=[pl.BlockSpec(memory_space=pltpu.SM...]
    ppermute x0 -> x2, starting transfers between devices: none -> 16.2 us  [the longest x1 9.04 us: per_device(): pair = (keep + lax.ppermute(give, 'outer', siblings)).astype(BF16)]
  transfers between devices with their start and end apart: 3 -> 6, of which waited for: 3 -> 5; matrix products, arithmetic and copies ran while one was open for 0% -> 1% of each run, Pallas kernels for 0% -> 6%
where the time goes in v2:
time: 139 us
  blocking collectives  51 us (37%)
  starting transfers between devices  28.3 us (20%)
  waiting for transfers between devices  24.3 us (17%)
  Pallas kernels  17.8 us (13%)
  between operations  14.8 us (11%)
  local copies, waits for them, and re-layouts  2.36 us (2%)
    all_to_all x1, blocking collectives, per_device(): lax.all_to_all(spread(mine, n_out // 2), 'outer', 0, 0, axis_index_groups...  22.9 us
    all_to_all x1, blocking collectives, per_device(): near = lax.all_to_all(spread(mine, n_in), 'inner', 0, 0)  16.2 us
    all_to_all x1, blocking collectives, per_device(): got = lax.all_to_all(pair, 'inner', 0, 0)  11.8 us
    all_to_all x1, waiting for transfers between devices, per_device(): lax.all_to_all(spread(mine, len(plane[0])), both_axes, 0, 0, axis_index_g...  9.32 us
    ppermute x1, starting transfers between devices, per_device(): pair = (keep + lax.ppermute(give, 'outer', siblings)).astype(BF16)  9.04 us
    ppermute x1, starting transfers between devices, per_device(): far = lax.ppermute(near, 'outer', siblings)  7.18 us
    pallas_call x1, Pallas kernels, first_part(): pl.pallas_call(first_kernel, in_specs=[pl.BlockSpec(memory_space=pltpu.SM...  6.88 us
    all_to_all x1, waiting for transfers between devices, per_device(): got = lax.all_to_all(tiles, both_axes, 0, 0, axis_index_groups=column)  6.2 us
  transfers between devices with their start and end apart: 6, of which 5 were waited for; matrix products, arithmetic and copies ran while one was open for 1% of the time, Pallas kernels for 6%

profile of v2, /device:TPU:1, one launch (start us, length us, event | category | flops | bytes accessed | tf_op | source)
XLA Modules:
  0.0 138.7 jit_solution(16809640131698363108)
XLA Ops:
  7.2 0.0 reduce-scatter.2.cloned.1.call-start
  7.9 6.9 %first_part.1 = (f32[16,64,128]{2,1,0:T(8,128)S(1)}, f32[16,64,128]{2,1,0:T(8,128)S(1)}, bf16[16,512,256]{2,1,0:T(8,128)(2,1)}) custom-call(s32[1]{0:T(128)} %bitcast.7.seed_ref, bf16[384,512]{1,0:T(8,128)(2,1)} %bitcast.14, f32[256,512]{1,0:T(8,128)} %bitcast.10, bf16[384,4096]{1,0:T(8,128)(2,1)} %bitcast.8), custom_call_target="tpu_custom_call" | custom-call | tf_op jit(solution)/shard_map/first_part/pallas_call | solution.py:109
  14.7 0.0 copy-start
  14.8 9.0 %collective-permute-start = (f32[16,64,128]{2,1,0:T(8,128)S(1)}, f32[16,64,128]{2,1,0:T(8,128)S(1)}, u32[]{:S(2)}, u32[]{:S(2)}) collective-permute-start(f32[16,64,128]{2,1,0:T(8,128)S(1)} %get-tuple-element.17), channel_id=1, source_target_pairs={{0,1},{1,0},{2,3},{3,2},{4,5},{5,4},{6,7},{7,6},{8,9},{9,8},{10,11... | collective-permute-start | bytes 1572872 | tf_op jit(solution)/shard_map/left_sum/ppermute | solution.py:286
  23.8 1.5 %collective-permute-done = f32[16,64,128]{2,1,0:T(8,128)S(1)} collective-permute-done((f32[16,64,128]{2,1,0:T(8,128)S(1)}, f32[16,64,128]{2,1,0:T(8,128)S(1)}, u32[]{:S(2)}, u32[]{:S(2)}) %collective-permute-start) | collective-permute-done | bytes 524320 | tf_op jit(solution)/shard_map/left_sum/ppermute | solution.py:286
  25.3 0.1 add_convert_fusion
  25.4 11.8 %all_to_all.30 = bf16[16,64,128]{2,1,0:T(8,128)(2,1)S(1)} all-to-all(bf16[16,64,128]{2,1,0:T(8,128)(2,1)S(1)} %add_convert_fusion), channel_id=1, replica_groups=mesh['inner'=16,'outer'=32] {'inner'}, dimensions={0} | all-to-all | bytes 524288 | tf_op jit(solution)/shard_map/left_sum/all_to_all | solution.py:287
  37.3 0.0 reduce-scatter.2.cloned.1.call-update
  37.3 22.9 %all_to_all.31 = bf16[16,64,128]{2,1,0:T(8,128)(2,1)S(1)} all-to-all(bf16[16,64,128]{2,1,0:T(8,128)(2,1)S(1)} %broadcast_in_dim.10), channel_id=1, replica_groups={{0,2,4,6,8,10,12,14,16,18,20,22,24,26,28,30},{1,3,5,7,9,11,13,15,17,19,..., dimensions={0} | all-to-all | bytes 524288 | tf_op jit(solution)/shard_map/left_sum/all_to_all | solution.py:290
  60.4 16.2 %all_to_all.32.near_ref = bf16[16,64,128]{2,1,0:T(8,128)(2,1)S(1)} all-to-all(bf16[16,64,128]{2,1,0:T(8,128)(2,1)S(1)} %broadcast_in_dim.11), channel_id=1, replica_groups=mesh['inner'=16,'outer'=32] {'inner'}, dimensions={0} | all-to-all | bytes 524288 | tf_op jit(solution)/shard_map/left_gather/all_to_all | solution.py:295
  76.6 7.2 %collective-permute-start.1 = (bf16[16,64,128]{2,1,0:T(8,128)(2,1)S(1)}, bf16[16,64,128]{2,1,0:T(8,128)(2,1)S(1)}, u32[]{:S(2)}, u32[]{:S(2)}) collective-permute-start(bf16[16,64,128]{2,1,0:T(8,128)(2,1)S(1)} %all_to_all.32.near_ref), channel_id=1, source_target_pairs={{0,1},{1,0},{2,3},{3,2},{4,5},{5,4},{6,7},{7,6},{8,9},{9,8},{10,11... | collective-permute-start | bytes 786440 | tf_op jit(solution)/shard_map/left_gather/ppermute | solution.py:296
  83.8 1.1 collective-permute-done.1.far_ref
  84.9 0.0 copy-done
  84.9 0.0 copy-start.1
  84.9 3.3 %right_part.1 = (bf16[16,16,128]{2,1,0:T(8,128)(2,1)}, f32[64,128]{1,0:T(8,128)S(1)}) custom-call(bf16[16,64,128]{2,1,0:T(8,128)(2,1)S(1)} %all_to_all.32.near_ref, bf16[16,64,128]{2,1,0:T(8,128)(2,1)S(1)} %collective-permute-done.1.far_ref, bf16[384,4096]{1,0:T(8,128)(2,1)S(1)} %bitcast.9, bf16[384,512]{1,0:T(8,128)(2,1)} %bitcast.15, f32[256,512]{1,0:T(8,128)} %bitcast.11), custom_call_target="tpu_custom_call" | custom-call | tf_op jit(solution)/shard_map/right_part/pallas_call | solution.py:163
  88.2 0.0 copy-done.1
  88.2 3.7 %all-to-all-start.3 = ((bf16[16,16,128]{2,1,0:T(8,128)(2,1)}), bf16[16,16,128]{2,1,0:T(8,128)(2,1)S(1)}, u32[]{:S(2)}, u32[]{:S(2)}) async-start(bf16[16,16,128]{2,1,0:T(8,128)(2,1)} %get-tuple-element.20), calls=%async_computation.3 | async-start | bytes 131072 | tf_op jit(solution)/shard_map/right_sum/all_to_all | solution.py:302
  91.9 1.6 %factor_a.1.aug_ref = f32[64,128]{1,0:T(8,128)S(1)} custom-call(f32[64,128]{1,0:T(8,128)S(1)} %get-tuple-element.19.aug_ref), custom_call_target="tpu_custom_call" | custom-call | flops 4000000 | bytes 2000000 | tf_op jit(solution)/shard_map/right_sum/factor_a/pallas_call | solution.py:199
  93.5 6.2 %all-to-all-done.3 = bf16[16,16,128]{2,1,0:T(8,128)(2,1)S(1)} async-done(((bf16[16,16,128]{2,1,0:T(8,128)(2,1)}), bf16[16,16,128]{2,1,0:T(8,128)(2,1)S(1)}, u32[]{:S(2)}, u32[]{:S(2)}) %all-to-all-start.3) | async-done | bytes 65568 | tf_op jit(solution)/shard_map/right_sum/all_to_all | solution.py:302
  99.8 0.7 broadcast_in_dim.12
  100.4 3.9 %all-to-all-start.4 = ((bf16[32,16,128]{2,1,0:T(8,128)(2,1)}), bf16[32,16,128]{2,1,0:T(8,128)(2,1)S(1)}, u32[]{:S(2)}, u32[]{:S(2)}) async-start(bf16[32,16,128]{2,1,0:T(8,128)(2,1)} %broadcast_in_dim.12), calls=%async_computation.4 | async-start | bytes 262144 | tf_op jit(solution)/shard_map/right_sum/all_to_all | solution.py:306
  104.3 1.8 %factor_b.1.aug_ref = f32[64,128]{1,0:T(8,128)S(1)} custom-call(f32[64,128]{1,0:T(8,128)S(1)} %factor_a.1.aug_ref), custom_call_target="tpu_custom_call" | custom-call | flops 4000000 | bytes 2000000 | tf_op jit(solution)/shard_map/right_sum/factor_b/pallas_call | solution.py:199
  106.1 9.3 %all-to-all-done.4 = bf16[32,16,128]{2,1,0:T(8,128)(2,1)S(1)} async-done(((bf16[32,16,128]{2,1,0:T(8,128)(2,1)}), bf16[32,16,128]{2,1,0:T(8,128)(2,1)S(1)}, u32[]{:S(2)}, u32[]{:S(2)}) %all-to-all-start.4) | async-done | bytes 131104 | tf_op jit(solution)/shard_map/right_sum/all_to_all | solution.py:306
  115.5 0.6 broadcast_in_dim.13
  116.1 4.5 %all-to-all-start.5 = ((bf16[16,16,128]{2,1,0:T(8,128)(2,1)}), bf16[16,16,128]{2,1,0:T(8,128)(2,1)S(1)}, u32[]{:S(2)}, u32[]{:S(2)}) async-start(bf16[16,16,128]{2,1,0:T(8,128)(2,1)} %broadcast_in_dim.13), calls=%async_computation.5 | async-start | bytes 131072 | tf_op jit(solution)/shard_map/right_sum/all_to_all | solution.py:310
  120.6 1.7 %factor_c.1.inv_ref = f32[64,128]{1,0:T(8,128)S(1)} custom-call(f32[64,128]{1,0:T(8,128)S(1)} %factor_b.1.aug_ref), custom_call_target="tpu_custom_call" | custom-call | flops 4000000 | bytes 2000000 | tf_op jit(solution)/shard_map/right_sum/factor_c/pallas_call | solution.py:199
  122.3 6.1 %all-to-all-done.5.tiles_ref = bf16[16,16,128]{2,1,0:T(8,128)(2,1)S(1)} async-done(((bf16[16,16,128]{2,1,0:T(8,128)(2,1)}), bf16[16,16,128]{2,1,0:T(8,128)(2,1)S(1)}, u32[]{:S(2)}, u32[]{:S(2)}) %all-to-all-start.5) | async-done | bytes 65568 | tf_op jit(solution)/shard_map/right_sum/all_to_all | solution.py:310
  128.4 0.0 reduce-scatter.2.cloned.1.call-done.grad_hbm
  128.4 0.0 copy-start.2
  128.4 0.9 copy-done.2
  129.4 2.5 %result.1 = (bf16[16,4096]{1,0:T(8,128)(2,1)}, f32[256,512]{1,0:T(8,128)}) custom-call(bf16[16,16,128]{2,1,0:T(8,128)(2,1)S(1)} %all-to-all-done.5.tiles_ref, f32[64,128]{1,0:T(8,128)S(1)} %factor_c.1.inv_ref, bf16[16,64,128]{2,1,0:T(8,128)(2,1)S(1)} %all_to_all.32.near_ref, bf16[16,64,128]{2,1,0:T(8,128)(2,1)S(1)} %copy-done.2, ...), custom_call_target="tpu_custom_call" | custom-call | tf_op jit(solution)/shard_map/result/pallas_call | solution.py:246
  (6 shorter events, 0.2 us)
Async XLA Ops:
  7.2 121.3 %reduce-scatter.2.cloned.1.call-start = ((), (), s32[]{:S(2)}) async-start(), calls=%async_computation.7 | async-start | bytes 4456448 | tf_op jit(solution)/shard_map/grad/reduce_scatter | solution.py:293
  14.7 70.2 %copy-start = (bf16[1,384,4096]{2,1,0:T(8,128)(2,1)S(1)}, bf16[1,384,4096]{2,1,0:T(8,128)(2,1)}, u32[]{:S(2)}) copy-start(bf16[1,384,4096]{2,1,0:T(8,128)(2,1)} %param.4) | copy-start | bytes 9437188
  14.8 10.6 %collective-permute-start = (f32[16,64,128]{2,1,0:T(8,128)S(1)}, f32[16,64,128]{2,1,0:T(8,128)S(1)}, u32[]{:S(2)}, u32[]{:S(2)}) collective-permute-start(f32[16,64,128]{2,1,0:T(8,128)S(1)} %get-tuple-element.17), channel_id=1, source_target_pairs={{0,1},{1,0},{2,3},{3,2},{4,5},{5,4},{6,7},{7,6},{8,9},{9,8},{10,11... | collective-permute-start | bytes 1572872 | tf_op jit(solution)/shard_map/left_sum/ppermute | solution.py:286
  76.6 8.3 %collective-permute-start.1 = (bf16[16,64,128]{2,1,0:T(8,128)(2,1)S(1)}, bf16[16,64,128]{2,1,0:T(8,128)(2,1)S(1)}, u32[]{:S(2)}, u32[]{:S(2)}) collective-permute-start(bf16[16,64,128]{2,1,0:T(8,128)(2,1)S(1)} %all_to_all.32.near_ref), channel_id=1, source_target_pairs={{0,1},{1,0},{2,3},{3,2},{4,5},{5,4},{6,7},{7,6},{8,9},{9,8},{10,11... | collective-permute-start | bytes 786440 | tf_op jit(solution)/shard_map/left_gather/ppermute | solution.py:296
  84.9 3.3 %copy-start.1 = (bf16[16,64,128]{2,1,0:T(8,128)(2,1)}, bf16[16,64,128]{2,1,0:T(8,128)(2,1)S(1)}, u32[]{:S(2)}) copy-start(bf16[16,64,128]{2,1,0:T(8,128)(2,1)S(1)} %collective-permute-done.1.far_ref) | copy-start | bytes 786436
  88.2 11.5 %all-to-all-start.3 = ((bf16[16,16,128]{2,1,0:T(8,128)(2,1)}), bf16[16,16,128]{2,1,0:T(8,128)(2,1)S(1)}, u32[]{:S(2)}, u32[]{:S(2)}) async-start(bf16[16,16,128]{2,1,0:T(8,128)(2,1)} %get-tuple-element.20), calls=%async_computation.3 | async-start | bytes 131072 | tf_op jit(solution)/shard_map/right_sum/all_to_all | solution.py:302
  100.4 15.0 %all-to-all-start.4 = ((bf16[32,16,128]{2,1,0:T(8,128)(2,1)}), bf16[32,16,128]{2,1,0:T(8,128)(2,1)S(1)}, u32[]{:S(2)}, u32[]{:S(2)}) async-start(bf16[32,16,128]{2,1,0:T(8,128)(2,1)} %broadcast_in_dim.12), calls=%async_computation.4 | async-start | bytes 262144 | tf_op jit(solution)/shard_map/right_sum/all_to_all | solution.py:306
  116.1 12.3 %all-to-all-start.5 = ((bf16[16,16,128]{2,1,0:T(8,128)(2,1)}), bf16[16,16,128]{2,1,0:T(8,128)(2,1)S(1)}, u32[]{:S(2)}, u32[]{:S(2)}) async-start(bf16[16,16,128]{2,1,0:T(8,128)(2,1)} %broadcast_in_dim.13), calls=%async_computation.5 | async-start | bytes 131072 | tf_op jit(solution)/shard_map/right_sum/all_to_all | solution.py:310
  128.4 1.0 copy-start.2
Sparse Core Ops, SparseCore 0:
  37.4 80.2 reduce-scatter.1

commit v3 on v2

--- a/solution.py
+++ b/solution.py
@@ -13,7 +13,6 @@
 F32 = jnp.float32
 BF16 = jnp.bfloat16
 MIB = 1024 * 1024
-CUTS = (20, 42)
 
 
 def seeded_start_t(seed, width):
@@ -41,6 +40,23 @@
 NN = ((1,), (0,))
 NT = ((1,), (1,))
 TN = ((0,), (0,))
+
+
+def factor_kernel(gram_ref, out_ref):
+    *_, out_ref[...] = elimination(gram_ref[...])
+
+
+def factor(gram):
+    vmem = pl.BlockSpec(memory_space=pltpu.VMEM)
+    return pl.pallas_call(
+        factor_kernel,
+        in_specs=[vmem],
+        out_specs=vmem,
+        out_shape=pltpu.VMEM((RANK, RANK), F32),
+        compiler_params=pltpu.CompilerParams(vmem_limit_bytes=4 * MIB),
+        cost_estimate=pl.CostEstimate(flops=4_000_000, bytes_accessed=2_000_000, transcendentals=0),
+        name="factor",
+    )(gram)
 
 
 def position():
@@ -75,10 +91,6 @@
     vs_t = parts[:RANK] + parts[RANK : 2 * RANK] + parts[2 * RANK :]
     v_t = v_ref[...].astype(F32).T.astype(BF16)
     lhs = jnp.concatenate(terms(vs_t, 2) + [v_t], 0)
-    c_copy.wait()
-    c_2 = terms(c_ref[...], 2)
-    cs = dot(start_3, c_2[0], NT) + dot(start_3, c_2[1], NT)
-    cs = cs[:RANK] + cs[RANK : 2 * RANK] + cs[2 * RANK :]
     per = wide // (2 * LANES)
     out_copies = []
     for j in range(count):
@@ -88,13 +100,20 @@
         for n in range(per):
             k = j * per + n
             cols = slice(2 * n * LANES, 2 * (n + 1) * LANES)
-            block = left[:, cols] + (inner == k).astype(F32) * cs
+            block = left[:, cols]
             even, odd = block[:, :LANES], block[:, LANES:]
             keep_ref[k] = jnp.where(core == 0, even, odd)
             give_ref[k] = jnp.where(core == 0, odd, even)
             part_ref[k] = both[2 * RANK :, cols].astype(BF16)
         span = pl.ds(j * per, per)
         out_copies += fetch([(part_ref.at[span], part_hbm.at[span])], out_sems.at[pl.ds(j, 1)])
+    c_copy.wait()
+    c_2 = terms(c_ref[...], 2)
+    cs = dot(start_3, c_2[0], NT) + dot(start_3, c_2[1], NT)
+    cs = cs[:RANK] + cs[RANK : 2 * RANK] + cs[2 * RANK :]
+    even, odd = cs[:, :LANES], cs[:, LANES:]
+    keep_ref[inner] += jnp.where(core == 0, even, odd)
+    give_ref[inner] += jnp.where(core == 0, odd, even)
     for copy in out_copies:
         copy.wait()
 
@@ -102,7 +121,7 @@
 def first_part(seed, v, c, x, n_in):
     tokens, feats = x.shape
     width = v.shape[1]
-    count = 8
+    count = 4
     vmem, hbm = pl.BlockSpec(memory_space=pltpu.VMEM), pl.BlockSpec(memory_space=pltpu.HBM)
     out = pltpu.VMEM((n_in, RANK, LANES), F32)
     part = pltpu.HBM((n_in, width, 2 * LANES), BF16)
@@ -130,25 +149,58 @@
     return jnp.concatenate([jnp.where(first, near, far), jnp.where(first, far, near)], 1).astype(BF16)
 
 
-def right_kernel(near_ref, far_ref, x_ref, v_hbm, c_hbm, out_ref, aug_ref, v_ref, c_ref, sems):
+def elimination(gram):
+    shape = (RANK, 2 * RANK)
+    eye = lax.broadcasted_iota(jnp.int32, shape, 0) == lax.broadcasted_iota(jnp.int32, shape, 1)
+    aug = jnp.concatenate([gram, eye[:, :RANK].astype(F32)], 1)
+    blocks = [aug[8 * k : 8 * k + 8] for k in range(RANK // 8)]
+    tile = blocks[0].shape
+    sub = lax.broadcasted_iota(jnp.int32, tile, 0)
+    full = lambda a: jnp.broadcast_to(a, tile)
+    for j in range(0, RANK, 2):
+        at, s = divmod(j, 8)
+        row_0, row_1 = full(blocks[at][s : s + 1]), full(blocks[at][s + 1 : s + 2])
+        a, b = full(row_0[:, j : j + 1]), full(row_0[:, j + 1 : j + 2])
+        c = full(row_1[:, j + 1 : j + 2])
+        over_a = 1.0 / a
+        ratio = b * over_a
+        scaled_0 = row_0 * over_a
+        scaled_1 = (row_1 - ratio * row_0) / (c - ratio * b)
+        for k in range(at, len(blocks)):
+            col_0 = full(blocks[k][:, j : j + 1])
+            col_1 = full(blocks[k][:, j + 1 : j + 2]) - col_0 * ratio
+            if k == at:
+                col_0, col_1 = jnp.where(sub > s, col_0, 0.0), jnp.where(sub > s + 1, col_1, 0.0)
+            blocks[k] = blocks[k] - col_0 * scaled_0 - col_1 * scaled_1
+        yield None
+    aug = jnp.concatenate(blocks, 0)
+    pivots = jnp.sum(jnp.where(eye, aug, 0.0), 1, keepdims=True)
+    yield aug[:, RANK:] * lax.rsqrt(pivots)
+
+
+def right_kernel(near_ref, far_ref, x_ref, v_hbm, c_hbm, out_ref, inv_ref, v_ref, c_ref, sems):
     inner, _, core = position()
     copies = fetch([(v_hbm, v_ref), (c_hbm, c_ref)], sems)
-    y = gram = 0.0
     per = 2
-    for k in range(0, near_ref.shape[0], per):
-        left = jnp.concatenate([in_order(core, near_ref[k + n], far_ref[k + n]) for n in range(per)], 1)
-        y += dot(x_ref[:, 2 * k * LANES : 2 * (k + per) * LANES], left, NT)
+    lefts = [
+        jnp.concatenate([in_order(core, near_ref[k + n], far_ref[k + n]) for n in range(per)], 1)
+        for k in range(0, near_ref.shape[0], per)
+    ]
+    gram = 0.0
+    for left in lefts:
         gram += dot(left, left, NT)
-    eye = lax.broadcasted_iota(jnp.int32, gram.shape, 0) == lax.broadcasted_iota(jnp.int32, gram.shape, 1)
-    aug_ref[...] = jnp.concatenate([gram, eye.astype(F32)], 1)
+    for copy in copies:
+        copy.wait()
+    y = 0.0
+    for k, left in enumerate(lefts):
+        y += dot(x_ref[:, 2 * k * per * LANES : 2 * (k + 1) * per * LANES], left, NT)
     y_2 = jnp.concatenate(terms(y.T, 2), 0)
     own = in_order(core, near_ref[inner], far_ref[inner])
-    for copy in copies:
-        copy.wait()
     both = dot(y_2, v_ref[...], NN)
     m = both[:RANK] + both[RANK:]
     for term in terms(c_ref[...], 2):
         m += dot(own, term, NN)
+    inv_ref[...] = gram
     high = out_ref.shape[1]
     across = m.shape[1] // LANES
     for k in range(out_ref.shape[0]):
@@ -164,65 +216,30 @@
         right_kernel,
         in_specs=[vmem, vmem, vmem, hbm, hbm],
         out_specs=[vmem, vmem],
-        out_shape=[jax.ShapeDtypeStruct((tiles, high, LANES), BF16), pltpu.VMEM((RANK, 2 * RANK), F32)],
+        out_shape=[jax.ShapeDtypeStruct((tiles, high, LANES), BF16), pltpu.VMEM((RANK, RANK), F32)],
         scratch_shapes=[pltpu.VMEM(v.shape, BF16), pltpu.VMEM(c.shape, F32), pltpu.SemaphoreType.DMA((2,))],
         compiler_params=pltpu.CompilerParams(vmem_limit_bytes=12 * MIB),
         name="right_part",
     )(in_vmem(near), in_vmem(far), x, in_hbm(v), in_hbm(c))
 
 
-def eliminate(aug, begin, end):
-    blocks = [aug[8 * k : 8 * k + 8] for k in range(RANK // 8)]
-    below = lax.broadcasted_iota(jnp.int32, blocks[0].shape, 0)
-    for j in range(begin, end):
-        at, sub = divmod(j, 8)
-        row = blocks[at][sub : sub + 1]
-        scaled = row / row[:, j : j + 1]
-        for k in range(at, len(blocks)):
-            taken = blocks[k][:, j : j + 1] * scaled
-            blocks[k] = blocks[k] - (jnp.where(below > sub, taken, 0.0) if k == at else taken)
-    return jnp.concatenate(blocks, 0)
-
-
-def more_kernel(begin, end, aug_ref, out_ref):
-    aug = eliminate(aug_ref[...], begin, end)
-    if end == RANK:
-        shape = (RANK, 2 * RANK)
-        eye = lax.broadcasted_iota(jnp.int32, shape, 0) == lax.broadcasted_iota(jnp.int32, shape, 1)
-        pivots = jnp.sum(jnp.where(eye, aug, 0.0), 1, keepdims=True)
-        aug = aug * lax.rsqrt(pivots)
-    out_ref[...] = aug
-
-
-def more_call(begin, end, name, aug):
-    vmem = pl.BlockSpec(memory_space=pltpu.VMEM)
-    return pl.pallas_call(
-        functools.partial(more_kernel, begin, end),
-        in_specs=[vmem],
-        out_specs=vmem,
-        out_shape=pltpu.VMEM(aug.shape, F32),
-        compiler_params=pltpu.CompilerParams(vmem_limit_bytes=4 * MIB),
-        cost_estimate=pl.CostEstimate(flops=4_000_000, bytes_accessed=2_000_000, transcendentals=0),
-        name=name,
-    )(aug)
-
-
-def result_kernel(n_out, tiles_ref, inv_ref, near_ref, far_ref, grad_hbm, c_hbm, update_hbm, new_hbm, update_ref, new_ref, grad_ref, c_ref, in_sems, out_sems):
-    copies = fetch([(grad_hbm, grad_ref), (c_hbm, c_ref)], in_sems)
+def result_kernel(n_out, tiles_ref, inv_ref, near_ref, far_hbm, grad_hbm, c_hbm, update_hbm, new_hbm, update_ref, new_ref, far_ref, grad_ref, c_ref, in_sems, out_sems):
+    copies = fetch([(far_hbm, far_ref), (grad_hbm, grad_ref), (c_hbm, c_ref)], in_sems)
     inner, outer, core = position()
     high = tiles_ref.shape[1]
     across = tiles_ref.shape[0] * high // RANK
     m_t = jnp.concatenate(
         [jnp.concatenate([tiles_ref[r * across + q] for q in range(across)], 1) for r in range(RANK // high)], 0
     ).astype(F32)
-    inv = inv_ref[:, RANK:]
+    inv = inv_ref[...]
     right_t = dot(inv, m_t, NN, precision=HI) / n_out
     q = dot(inv, right_t, TN, precision=HI)
     q_2 = terms(q, 2)
+    copies[0].wait()
     own = in_order(core, near_ref[inner], far_ref[inner])
     approx = dot(jnp.concatenate([own, own], 0), jnp.concatenate(q_2, 0), TN)
-    for copy in copies:
-        copy.wait()
+    copies[1].wait()
+    copies[2].wait()
     new_ref[...] = grad_ref[...].astype(F32).T + c_ref[...] - approx
     rows = new_ref.shape[0] // 2
     out = [(new_ref.at[pl.ds(k * rows, rows)], new_hbm.at[pl.ds(k * rows, rows)]) for k in range(2)]
@@ -245,20 +262,21 @@
     update = jax.ShapeDtypeStruct((c.shape[1] // n_out, near.shape[0] * 2 * LANES), BF16)
     return pl.pallas_call(
         functools.partial(result_kernel, n_out),
-        in_specs=[vmem] * 4 + [hbm] * 2,
+        in_specs=[vmem] * 3 + [hbm] * 3,
         out_specs=[hbm, hbm],
         out_shape=[update, jax.ShapeDtypeStruct(c.shape, F32)],
         scratch_shapes=[
             pltpu.VMEM(update.shape, BF16),
             pltpu.VMEM(c.shape, F32),
+            pltpu.VMEM(far.shape, BF16),
             pltpu.VMEM(grad_t.shape, BF16),
             pltpu.VMEM(c.shape, F32),
-            pltpu.SemaphoreType.DMA((2,)),
+            pltpu.SemaphoreType.DMA((3,)),
             pltpu.SemaphoreType.DMA((3,)),
         ],
         compiler_params=pltpu.CompilerParams(vmem_limit_bytes=12 * MIB),
         name="result",
-    )(tiles, inv, in_vmem(near), in_vmem(far), in_hbm(grad_t), in_hbm(c))
+    )(tiles, inv, in_vmem(near), in_hbm(far), in_hbm(grad_t), in_hbm(c))
 
 
 def spread(piece, count):
@@ -294,19 +312,15 @@
     with jax.named_scope("left_gather"):
         near = lax.all_to_all(spread(mine, n_in), "inner", 0, 0)
         far = lax.ppermute(near, "outer", siblings)
-    tiles, aug = right_part(near, far, v, c, x)
+    tiles, inv = right_part(near, far, v, c, x)
+    inv = factor(inv)
     with jax.named_scope("right_sum"):
         both_axes = ("inner", "outer")
         column, plane = chip_groups(n_in, n_out)
-        aug = more_call(0, CUTS[0], "factor_a", aug)
         got = lax.all_to_all(tiles, both_axes, 0, 0, axis_index_groups=column)
         mine = jnp.sum(got.astype(F32), 0).astype(BF16)
-        aug, mine = lax.optimization_barrier((aug, mine))
-        aug = more_call(CUTS[0], CUTS[1], "factor_b", aug)
         got = lax.all_to_all(spread(mine, len(plane[0])), both_axes, 0, 0, axis_index_groups=plane)
         mine = jnp.sum(got.astype(F32), 0).astype(BF16)
-        aug, mine = lax.optimization_barrier((aug, mine))
-        inv = more_call(CUTS[1], RANK, "factor_c", aug)
         tiles = lax.all_to_all(spread(mine, len(column[0])), both_axes, 0, 0, axis_index_groups=column)
     update_t, new_carried = result(tiles, inv, near, far, grad_t, c, n_out)
     return (update_t.T, new_carried[None])

time: 139 us -> 136 us (0.978)
  blocking collectives: 51 us -> 76.1 us
  waiting for transfers between devices: 24.3 us -> 5.7 us
  starting transfers between devices: 28.3 us -> 21.6 us
  Pallas kernels: 17.8 us -> 16.2 us
  local copies, waits for them, and re-layouts: 2.36 us -> 0.76 us
    all_to_all x0 -> x2, blocking collectives: none -> 25.5 us  [the longest x1 14.9 us: per_device(): lax.all_to_all(spread(mine, len(plane[0])), both_axes, 0, 0, axis_index_g...]
    all_to_all x2 -> x0, waiting for transfers between devices: 15.5 us -> none  [the longest x1 9.32 us: per_device(): lax.all_to_all(spread(mine, len(plane[0])), both_axes, 0, 0, axis_index_g...]
    all_to_all x2 -> x0, starting transfers between devices: 7.53 us -> none  [the longest x1 3.86 us: per_device(): lax.all_to_all(spread(mine, len(plane[0])), both_axes, 0, 0, axis_index_g...]
    all_to_all x1, waiting for transfers between devices: 6.11 us -> 3.02 us  [per_device(): lax.all_to_all(spread(mine, len(column[0])), both_axes, 0, 0, axis_index_...]
    pallas_call x3 -> x1, Pallas kernels: 5.16 us -> 4.81 us  [factor(): pl.pallas_call(factor_kernel, in_specs=[vmem], out_specs=vmem, out_shape=...]
  transfers between devices with their start and end apart: 6 -> 4, of which waited for: 5 -> 3; matrix products, arithmetic and copies ran while one was open for 1% -> 1% of each run, Pallas kernels for 6% -> 6%
where the time goes in v3:
time: 136 us; the launch traced here: 135 us
  blocking collectives  76.1 us (56%)
  starting transfers between devices  21.6 us (16%)
  Pallas kernels  16.2 us (12%)
  between operations  14.8 us (11%)
  waiting for transfers between devices  5.7 us (4%)
    all_to_all x1, blocking collectives, per_device(): lax.all_to_all(spread(mine, n_out // 2), 'outer', 0, 0, axis_index_groups...  22.9 us
    all_to_all x1, blocking collectives, per_device(): near = lax.all_to_all(spread(mine, n_in), 'inner', 0, 0)  15.8 us
    all_to_all x1, blocking collectives, per_device(): lax.all_to_all(spread(mine, len(plane[0])), both_axes, 0, 0, axis_index_g...  14.9 us
    all_to_all x1, blocking collectives, per_device(): got = lax.all_to_all(pair, 'inner', 0, 0)  11.8 us
    all_to_all x1, blocking collectives, per_device(): got = lax.all_to_all(tiles, both_axes, 0, 0, axis_index_groups=column)  10.6 us
    ppermute x1, starting transfers between devices, per_device(): pair = (keep + lax.ppermute(give, 'outer', siblings)).astype(BF16)  9.06 us
    ppermute x1, starting transfers between devices, per_device(): far = lax.ppermute(near, 'outer', siblings)  7.44 us
    pallas_call x1, Pallas kernels, first_part(): pl.pallas_call(first_kernel, in_specs=[pl.BlockSpec(memory_space=pltpu.SM...  5.98 us
  transfers between devices with their start and end apart: 4, of which 3 were waited for; matrix products, arithmetic and copies ran while one was open for 1% of the time, Pallas kernels for 6%

profile of v3, /device:TPU:1, one launch (start us, length us, event | category | flops | bytes accessed | tf_op | source)
XLA Modules:
  0.0 135.3 jit_solution(13772846132425794837)
XLA Ops:
  7.2 0.0 reduce-scatter.2.cloned.1.call-start
  7.9 6.0 %first_part.1 = (f32[16,64,128]{2,1,0:T(8,128)S(1)}, f32[16,64,128]{2,1,0:T(8,128)S(1)}, bf16[16,512,256]{2,1,0:T(8,128)(2,1)}) custom-call(s32[1]{0:T(128)} %bitcast.7.seed_ref, bf16[384,512]{1,0:T(8,128)(2,1)} %bitcast.14, f32[256,512]{1,0:T(8,128)} %bitcast.10, bf16[384,4096]{1,0:T(8,128)(2,1)} %bitcast.8), custom_call_target="tpu_custom_call" | custom-call | tf_op jit(solution)/shard_map/first_part/pallas_call | solution.py:128
  13.8 0.0 copy-start
  13.9 9.1 %collective-permute-start = (f32[16,64,128]{2,1,0:T(8,128)S(1)}, f32[16,64,128]{2,1,0:T(8,128)S(1)}, u32[]{:S(2)}, u32[]{:S(2)}) collective-permute-start(f32[16,64,128]{2,1,0:T(8,128)S(1)} %get-tuple-element.13), channel_id=1, source_target_pairs={{0,1},{1,0},{2,3},{3,2},{4,5},{5,4},{6,7},{7,6},{8,9},{9,8},{10,11... | collective-permute-start | bytes 1572872 | tf_op jit(solution)/shard_map/left_sum/ppermute | solution.py:304
  22.9 1.5 %collective-permute-done = f32[16,64,128]{2,1,0:T(8,128)S(1)} collective-permute-done((f32[16,64,128]{2,1,0:T(8,128)S(1)}, f32[16,64,128]{2,1,0:T(8,128)S(1)}, u32[]{:S(2)}, u32[]{:S(2)}) %collective-permute-start) | collective-permute-done | bytes 524320 | tf_op jit(solution)/shard_map/left_sum/ppermute | solution.py:304
  24.4 0.1 add_convert_fusion
  24.5 11.8 %all_to_all.30 = bf16[16,64,128]{2,1,0:T(8,128)(2,1)S(1)} all-to-all(bf16[16,64,128]{2,1,0:T(8,128)(2,1)S(1)} %add_convert_fusion), channel_id=1, replica_groups=mesh['inner'=16,'outer'=32] {'inner'}, dimensions={0} | all-to-all | bytes 524288 | tf_op jit(solution)/shard_map/left_sum/all_to_all | solution.py:305
  36.4 0.0 reduce-scatter.2.cloned.1.call-update
  36.5 22.9 %all_to_all.31 = bf16[16,64,128]{2,1,0:T(8,128)(2,1)S(1)} all-to-all(bf16[16,64,128]{2,1,0:T(8,128)(2,1)S(1)} %broadcast_in_dim.10), channel_id=1, replica_groups={{0,2,4,6,8,10,12,14,16,18,20,22,24,26,28,30},{1,3,5,7,9,11,13,15,17,19,..., dimensions={0} | all-to-all | bytes 524288 | tf_op jit(solution)/shard_map/left_sum/all_to_all | solution.py:308
  59.5 15.8 %all_to_all.32.near_ref = bf16[16,64,128]{2,1,0:T(8,128)(2,1)S(1)} all-to-all(bf16[16,64,128]{2,1,0:T(8,128)(2,1)S(1)} %broadcast_in_dim.11), channel_id=1, replica_groups=mesh['inner'=16,'outer'=32] {'inner'}, dimensions={0} | all-to-all | bytes 524288 | tf_op jit(solution)/shard_map/left_gather/all_to_all | solution.py:313
  75.3 7.4 %collective-permute-start.1 = (bf16[16,64,128]{2,1,0:T(8,128)(2,1)S(1)}, bf16[16,64,128]{2,1,0:T(8,128)(2,1)S(1)}, u32[]{:S(2)}, u32[]{:S(2)}) collective-permute-start(bf16[16,64,128]{2,1,0:T(8,128)(2,1)S(1)} %all_to_all.32.near_ref), channel_id=1, source_target_pairs={{0,1},{1,0},{2,3},{3,2},{4,5},{5,4},{6,7},{7,6},{8,9},{9,8},{10,11... | collective-permute-start | bytes 786440 | tf_op jit(solution)/shard_map/left_gather/ppermute | solution.py:314
  82.7 1.1 collective-permute-done.1.far_ref.far_hbm
  83.9 0.0 copy-done
  83.9 0.0 copy-start.1
  83.9 2.9 %right_part.1 = (bf16[16,16,128]{2,1,0:T(8,128)(2,1)S(1)}, f32[64,64]{1,0:T(8,128)S(1)}) custom-call(bf16[16,64,128]{2,1,0:T(8,128)(2,1)S(1)} %all_to_all.32.near_ref, bf16[16,64,128]{2,1,0:T(8,128)(2,1)S(1)} %collective-permute-done.1.far_ref.far_hbm, bf16[384,4096]{1,0:T(8,128)(2,1)S(1)} %bitcast.9, bf16[384,512]{1,0:T(8,128)(2,1)} %bitcast.15, ...), custom_call_target="tpu_custom_call" | custom-call | tf_op jit(solution)/shard_map/right_part/pallas_call | solution.py:215
  86.8 0.0 copy-done.1
  86.8 10.6 %all_to_all.33 = bf16[16,16,128]{2,1,0:T(8,128)(2,1)S(1)} all-to-all(bf16[16,16,128]{2,1,0:T(8,128)(2,1)S(1)} %get-tuple-element.15), channel_id=1, replica_groups={{0,1,4,5,8,9,12,13,16,17,20,21,24,25,28,29},{2,3,6,7,10,11,14,15,18,19,..., dimensions={0} | all-to-all | bytes 131072 | tf_op jit(solution)/shard_map/right_sum/all_to_all | solution.py:320
  97.4 14.9 %all_to_all.34 = bf16[32,16,128]{2,1,0:T(8,128)(2,1)S(1)} all-to-all(bf16[32,16,128]{2,1,0:T(8,128)(2,1)S(1)} %broadcast_in_dim.12), channel_id=1, replica_groups={{0,2,32,34,64,66,96,98,128,130,160,162,192,194,224,226,256,258,288,290,..., dimensions={0} | all-to-all | bytes 262144 | tf_op jit(solution)/shard_map/right_sum/all_to_all | solution.py:322
  112.4 0.6 broadcast_in_dim.13
  113.0 5.1 %all-to-all-start.5 = ((bf16[16,16,128]{2,1,0:T(8,128)(2,1)}), bf16[16,16,128]{2,1,0:T(8,128)(2,1)S(1)}, u32[]{:S(2)}, u32[]{:S(2)}) async-start(bf16[16,16,128]{2,1,0:T(8,128)(2,1)} %broadcast_in_dim.13), calls=%async_computation.5 | async-start | bytes 131072 | tf_op jit(solution)/shard_map/right_sum/all_to_all | solution.py:324
  118.1 4.8 %factor.1.inv_ref = f32[64,64]{1,0:T(8,128)S(1)} custom-call(f32[64,64]{1,0:T(8,128)S(1)} %get-tuple-element.16.gram_ref), custom_call_target="tpu_custom_call" | custom-call | flops 4000000 | bytes 2000000 | tf_op jit(solution)/shard_map/factor/pallas_call | solution.py:51
  122.9 3.0 %all-to-all-done.5.tiles_ref = bf16[16,16,128]{2,1,0:T(8,128)(2,1)S(1)} async-done(((bf16[16,16,128]{2,1,0:T(8,128)(2,1)}), bf16[16,16,128]{2,1,0:T(8,128)(2,1)S(1)}, u32[]{:S(2)}, u32[]{:S(2)}) %all-to-all-start.5) | async-done | bytes 65568 | tf_op jit(solution)/shard_map/right_sum/all_to_all | solution.py:324
  125.9 0.0 reduce-scatter.2.cloned.1.call-done.grad_hbm
  125.9 2.5 %result.1 = (bf16[16,4096]{1,0:T(8,128)(2,1)}, f32[256,512]{1,0:T(8,128)}) custom-call(bf16[16,16,128]{2,1,0:T(8,128)(2,1)S(1)} %all-to-all-done.5.tiles_ref, f32[64,64]{1,0:T(8,128)S(1)} %factor.1.inv_ref, bf16[16,64,128]{2,1,0:T(8,128)(2,1)S(1)} %all_to_all.32.near_ref, bf16[16,64,128]{2,1,0:T(8,128)(2,1)} %copy-done.1, ...), custom_call_target="tpu_custom_call" | custom-call | tf_op jit(solution)/shard_map/result/pallas_call | solution.py:263
  (7 shorter events, 0.3 us)
Async XLA Ops:
  7.2 118.8 %reduce-scatter.2.cloned.1.call-start = ((), (), s32[]{:S(2)}) async-start(), calls=%async_computation.7 | async-start | bytes 4456448 | tf_op jit(solution)/shard_map/grad/reduce_scatter | solution.py:311
  13.8 70.0 %copy-start = (bf16[1,384,4096]{2,1,0:T(8,128)(2,1)S(1)}, bf16[1,384,4096]{2,1,0:T(8,128)(2,1)}, u32[]{:S(2)}) copy-start(bf16[1,384,4096]{2,1,0:T(8,128)(2,1)} %param.4) | copy-start | bytes 9437188
  13.9 10.6 %collective-permute-start = (f32[16,64,128]{2,1,0:T(8,128)S(1)}, f32[16,64,128]{2,1,0:T(8,128)S(1)}, u32[]{:S(2)}, u32[]{:S(2)}) collective-permute-start(f32[16,64,128]{2,1,0:T(8,128)S(1)} %get-tuple-element.13), channel_id=1, source_target_pairs={{0,1},{1,0},{2,3},{3,2},{4,5},{5,4},{6,7},{7,6},{8,9},{9,8},{10,11... | collective-permute-start | bytes 1572872 | tf_op jit(solution)/shard_map/left_sum/ppermute | solution.py:304
  75.3 8.6 %collective-permute-start.1 = (bf16[16,64,128]{2,1,0:T(8,128)(2,1)S(1)}, bf16[16,64,128]{2,1,0:T(8,128)(2,1)S(1)}, u32[]{:S(2)}, u32[]{:S(2)}) collective-permute-start(bf16[16,64,128]{2,1,0:T(8,128)(2,1)S(1)} %all_to_all.32.near_ref), channel_id=1, source_target_pairs={{0,1},{1,0},{2,3},{3,2},{4,5},{5,4},{6,7},{7,6},{8,9},{9,8},{10,11... | collective-permute-start | bytes 786440 | tf_op jit(solution)/shard_map/left_gather/ppermute | solution.py:314
  83.9 2.9 %copy-start.1 = (bf16[16,64,128]{2,1,0:T(8,128)(2,1)}, bf16[16,64,128]{2,1,0:T(8,128)(2,1)S(1)}, u32[]{:S(2)}) copy-start(bf16[16,64,128]{2,1,0:T(8,128)(2,1)S(1)} %collective-permute-done.1.far_ref.far_hbm) | copy-start | bytes 786436
  113.0 12.9 %all-to-all-start.5 = ((bf16[16,16,128]{2,1,0:T(8,128)(2,1)}), bf16[16,16,128]{2,1,0:T(8,128)(2,1)S(1)}, u32[]{:S(2)}, u32[]{:S(2)}) async-start(bf16[16,16,128]{2,1,0:T(8,128)(2,1)} %broadcast_in_dim.13), calls=%async_computation.5 | async-start | bytes 131072 | tf_op jit(solution)/shard_map/right_sum/all_to_all | solution.py:324
Sparse Core Ops, SparseCore 0:
  36.5 79.6 reduce-scatter.1

commit v4 on v3

--- a/solution.py
+++ b/solution.py
@@ -283,40 +283,47 @@
     return jnp.broadcast_to(piece[None], (count,) + piece.shape)
 
 
-def chip_groups(n_in, n_out):
-    column, plane = {}, {}
+def grouped(n_in, n_out, key):
+    groups = {}
     for i in range(n_in * n_out):
         inner, outer = divmod(i, n_out)
-        z, x_hi, core = outer // 4, outer // 2 % 2, outer % 2
-        column.setdefault((inner, x_hi), []).append(i)
-        plane.setdefault((z, core), []).append(i)
-    return list(column.values()), list(plane.values())
+        x_lo, y = divmod(inner, n_in // 2)
+        place = x_lo, y, outer // 4, outer // 2 % 2, outer % 2
+        groups.setdefault(key(*place), []).append(i)
+    return list(groups.values())
+
+
+def exchange_groups(n_in, n_out):
+    first = grouped(n_in, n_out, lambda x_lo, y, z, x_hi, core: (core, x_hi, y if core else z))
+    second = grouped(n_in, n_out, lambda x_lo, y, z, x_hi, core: (core, x_lo, z if core else y))
+    column = grouped(n_in, n_out, lambda x_lo, y, z, x_hi, core: (x_lo, x_hi, y))
+    plane = grouped(n_in, n_out, lambda x_lo, y, z, x_hi, core: (z, core))
+    return first, second, column, plane
 
 
 def per_device(acts, grad_out, carried, start_seed):
     x, v, c = acts[0], grad_out[0], carried[0]
     n_in, n_out = lax.axis_size("inner"), lax.axis_size("outer")
     siblings = [(i, i ^ 1) for i in range(n_out)]
-    same_core = [[i for i in range(n_out) if i % 2 == k] for k in range(2)]
+    both_axes = ("inner", "outer")
+    first, second, column, plane = exchange_groups(n_in, n_out)
 
     keep, give, part = first_part(start_seed.reshape(1), v, c, x, n_in)
     with jax.named_scope("left_sum"):
         pair = (keep + lax.ppermute(give, "outer", siblings)).astype(BF16)
-        got = lax.all_to_all(pair, "inner", 0, 0)
+        got = lax.all_to_all(pair, both_axes, 0, 0, axis_index_groups=first)
         mine = jnp.sum(got.astype(F32), 0).astype(BF16)
         part, mine = lax.optimization_barrier((part, mine))
-        got = lax.all_to_all(spread(mine, n_out // 2), "outer", 0, 0, axis_index_groups=same_core)
+        got = lax.all_to_all(spread(mine, len(second[0])), both_axes, 0, 0, axis_index_groups=second)
         mine = jnp.sum(got.astype(F32), 0).astype(BF16)
     with jax.named_scope("grad"):
         grad_t = lax.psum_scatter(part.reshape(-1, part.shape[2]), "inner", scatter_dimension=0, tiled=True)
     with jax.named_scope("left_gather"):
-        near = lax.all_to_all(spread(mine, n_in), "inner", 0, 0)
+        near = lax.all_to_all(spread(mine, len(first[0])), both_axes, 0, 0, axis_index_groups=first)
         far = lax.ppermute(near, "outer", siblings)
     tiles, inv = right_part(near, far, v, c, x)
     inv = factor(inv)
     with jax.named_scope("right_sum"):
-        both_axes = ("inner", "outer")
-        column, plane = chip_groups(n_in, n_out)
         got = lax.all_to_all(tiles, both_axes, 0, 0, axis_index_groups=column)
         mine = jnp.sum(got.astype(F32), 0).astype(BF16)
         got = lax.all_to_all(spread(mine, len(plane[0])), both_axes, 0, 0, axis_index_groups=plane)

time: 136 us -> 132 us (0.971)
  blocking collectives: 76.1 us -> 72.2 us
    all_to_all x3, blocking collectives: 50.5 us -> 45.2 us  [the longest x1 20.5 us: per_device(): lax.all_to_all(spread(mine, len(second[0])), both_axes, 0, 0, axis_index_...]
where the time goes in v4:
time: 132 us; the launch traced here: 131 us
  blocking collectives  72.2 us (55%)
  starting transfers between devices  21.5 us (16%)
  Pallas kernels  16.2 us (12%)
  between operations  14.8 us (11%)
  waiting for transfers between devices  5.7 us (4%)
    all_to_all x1, blocking collectives, per_device(): lax.all_to_all(spread(mine, len(second[0])), both_axes, 0, 0, axis_index_...  20.5 us
    all_to_all x1, blocking collectives, per_device(): lax.all_to_all(spread(mine, len(plane[0])), both_axes, 0, 0, axis_index_g...  15.1 us
    all_to_all x1, blocking collectives, per_device(): got = lax.all_to_all(pair, both_axes, 0, 0, axis_index_groups=first)  13.2 us
    all_to_all x1, blocking collectives, per_device(): got = lax.all_to_all(tiles, both_axes, 0, 0, axis_index_groups=column)  11.9 us
    all_to_all x1, blocking collectives, per_device(): lax.all_to_all(spread(mine, len(first[0])), both_axes, 0, 0, axis_index_g...  11.5 us
    ppermute x1, starting transfers between devices, per_device(): pair = (keep + lax.ppermute(give, 'outer', siblings)).astype(BF16)  9.06 us
    ppermute x1, starting transfers between devices, per_device(): far = lax.ppermute(near, 'outer', siblings)  7.32 us
    pallas_call x1, Pallas kernels, first_part(): pl.pallas_call(first_kernel, in_specs=[pl.BlockSpec(memory_space=pltpu.SM...  5.98 us
  transfers between devices with their start and end apart: 4, of which 3 were waited for; matrix products, arithmetic and copies ran while one was open for 1% of the time, Pallas kernels for 6%

profile of v4, /device:TPU:1, one launch (start us, length us, event | category | flops | bytes accessed | tf_op | source)
XLA Modules:
  0.0 131.4 jit_solution(16407592412877681080)
XLA Ops:
  7.2 0.0 reduce-scatter.2.cloned.1.call-start
  7.9 6.0 %first_part.1 = (f32[16,64,128]{2,1,0:T(8,128)S(1)}, f32[16,64,128]{2,1,0:T(8,128)S(1)}, bf16[16,512,256]{2,1,0:T(8,128)(2,1)}) custom-call(s32[1]{0:T(128)} %bitcast.7.seed_ref, bf16[384,512]{1,0:T(8,128)(2,1)} %bitcast.14, f32[256,512]{1,0:T(8,128)} %bitcast.10, bf16[384,4096]{1,0:T(8,128)(2,1)} %bitcast.8), custom_call_target="tpu_custom_call" | custom-call | tf_op jit(solution)/shard_map/first_part/pallas_call | solution.py:128
  13.8 0.0 copy-start
  13.9 9.1 %collective-permute-start = (f32[16,64,128]{2,1,0:T(8,128)S(1)}, f32[16,64,128]{2,1,0:T(8,128)S(1)}, u32[]{:S(2)}, u32[]{:S(2)}) collective-permute-start(f32[16,64,128]{2,1,0:T(8,128)S(1)} %get-tuple-element.13), channel_id=1, source_target_pairs={{0,1},{1,0},{2,3},{3,2},{4,5},{5,4},{6,7},{7,6},{8,9},{9,8},{10,11... | collective-permute-start | bytes 1572872 | tf_op jit(solution)/shard_map/left_sum/ppermute | solution.py:313
  22.9 1.5 %collective-permute-done = f32[16,64,128]{2,1,0:T(8,128)S(1)} collective-permute-done((f32[16,64,128]{2,1,0:T(8,128)S(1)}, f32[16,64,128]{2,1,0:T(8,128)S(1)}, u32[]{:S(2)}, u32[]{:S(2)}) %collective-permute-start) | collective-permute-done | bytes 524320 | tf_op jit(solution)/shard_map/left_sum/ppermute | solution.py:313
  24.4 0.1 add_convert_fusion
  24.5 13.2 %all_to_all.30 = bf16[16,64,128]{2,1,0:T(8,128)(2,1)S(1)} all-to-all(bf16[16,64,128]{2,1,0:T(8,128)(2,1)S(1)} %add_convert_fusion), channel_id=1, replica_groups={{0,32,64,96,128,160,192,224,256,288,320,352,384,416,448,480},{1,5,9,13,..., dimensions={0} | all-to-all | bytes 524288 | tf_op jit(solution)/shard_map/left_sum/all_to_all | solution.py:314
  37.8 0.0 reduce-scatter.2.cloned.1.call-update
  37.9 20.5 %all_to_all.31 = bf16[16,64,128]{2,1,0:T(8,128)(2,1)S(1)} all-to-all(bf16[16,64,128]{2,1,0:T(8,128)(2,1)S(1)} %broadcast_in_dim.10), channel_id=1, replica_groups={{0,2,4,6,8,10,12,14,16,18,20,22,24,26,28,30},{1,3,33,35,65,67,97,99,129..., dimensions={0} | all-to-all | bytes 524288 | tf_op jit(solution)/shard_map/left_sum/all_to_all | solution.py:317
  58.4 11.5 %all_to_all.32.near_ref = bf16[16,64,128]{2,1,0:T(8,128)(2,1)S(1)} all-to-all(bf16[16,64,128]{2,1,0:T(8,128)(2,1)S(1)} %broadcast_in_dim.11), channel_id=1, replica_groups={{0,32,64,96,128,160,192,224,256,288,320,352,384,416,448,480},{1,5,9,13,..., dimensions={0} | all-to-all | bytes 524288 | tf_op jit(solution)/shard_map/left_gather/all_to_all | solution.py:322
  70.0 7.3 %collective-permute-start.1 = (bf16[16,64,128]{2,1,0:T(8,128)(2,1)S(1)}, bf16[16,64,128]{2,1,0:T(8,128)(2,1)S(1)}, u32[]{:S(2)}, u32[]{:S(2)}) collective-permute-start(bf16[16,64,128]{2,1,0:T(8,128)(2,1)S(1)} %all_to_all.32.near_ref), channel_id=1, source_target_pairs={{0,1},{1,0},{2,3},{3,2},{4,5},{5,4},{6,7},{7,6},{8,9},{9,8},{10,11... | collective-permute-start | bytes 786440 | tf_op jit(solution)/shard_map/left_gather/ppermute | solution.py:323
  77.3 1.1 collective-permute-done.1.far_ref.far_hbm
  78.4 0.0 copy-done
  78.4 0.0 copy-start.1
  78.4 2.9 %right_part.1 = (bf16[16,16,128]{2,1,0:T(8,128)(2,1)S(1)}, f32[64,64]{1,0:T(8,128)S(1)}) custom-call(bf16[16,64,128]{2,1,0:T(8,128)(2,1)S(1)} %all_to_all.32.near_ref, bf16[16,64,128]{2,1,0:T(8,128)(2,1)S(1)} %collective-permute-done.1.far_ref.far_hbm, bf16[384,4096]{1,0:T(8,128)(2,1)S(1)} %bitcast.9, bf16[384,512]{1,0:T(8,128)(2,1)} %bitcast.15, ...), custom_call_target="tpu_custom_call" | custom-call | tf_op jit(solution)/shard_map/right_part/pallas_call | solution.py:215
  81.3 0.0 copy-done.1
  81.3 11.9 %all_to_all.33 = bf16[16,16,128]{2,1,0:T(8,128)(2,1)S(1)} all-to-all(bf16[16,16,128]{2,1,0:T(8,128)(2,1)S(1)} %get-tuple-element.15), channel_id=1, replica_groups={{0,1,4,5,8,9,12,13,16,17,20,21,24,25,28,29},{2,3,6,7,10,11,14,15,18,19,..., dimensions={0} | all-to-all | bytes 131072 | tf_op jit(solution)/shard_map/right_sum/all_to_all | solution.py:327
  93.3 15.1 %all_to_all.34 = bf16[32,16,128]{2,1,0:T(8,128)(2,1)S(1)} all-to-all(bf16[32,16,128]{2,1,0:T(8,128)(2,1)S(1)} %broadcast_in_dim.12), channel_id=1, replica_groups={{0,2,32,34,64,66,96,98,128,130,160,162,192,194,224,226,256,258,288,290,..., dimensions={0} | all-to-all | bytes 262144 | tf_op jit(solution)/shard_map/right_sum/all_to_all | solution.py:329
  108.4 0.6 broadcast_in_dim.13
  109.1 5.1 %all-to-all-start.5 = ((bf16[16,16,128]{2,1,0:T(8,128)(2,1)}), bf16[16,16,128]{2,1,0:T(8,128)(2,1)S(1)}, u32[]{:S(2)}, u32[]{:S(2)}) async-start(bf16[16,16,128]{2,1,0:T(8,128)(2,1)} %broadcast_in_dim.13), calls=%async_computation.5 | async-start | bytes 131072 | tf_op jit(solution)/shard_map/right_sum/all_to_all | solution.py:331
  114.2 4.8 %factor.1.inv_ref = f32[64,64]{1,0:T(8,128)S(1)} custom-call(f32[64,64]{1,0:T(8,128)S(1)} %get-tuple-element.16.gram_ref), custom_call_target="tpu_custom_call" | custom-call | flops 4000000 | bytes 2000000 | tf_op jit(solution)/shard_map/factor/pallas_call | solution.py:51
  119.0 3.0 %all-to-all-done.5.tiles_ref = bf16[16,16,128]{2,1,0:T(8,128)(2,1)S(1)} async-done(((bf16[16,16,128]{2,1,0:T(8,128)(2,1)}), bf16[16,16,128]{2,1,0:T(8,128)(2,1)S(1)}, u32[]{:S(2)}, u32[]{:S(2)}) %all-to-all-start.5) | async-done | bytes 65568 | tf_op jit(solution)/shard_map/right_sum/all_to_all | solution.py:331
  122.0 0.0 reduce-scatter.2.cloned.1.call-done.grad_hbm
  122.0 2.5 %result.1 = (bf16[16,4096]{1,0:T(8,128)(2,1)}, f32[256,512]{1,0:T(8,128)}) custom-call(bf16[16,16,128]{2,1,0:T(8,128)(2,1)S(1)} %all-to-all-done.5.tiles_ref, f32[64,64]{1,0:T(8,128)S(1)} %factor.1.inv_ref, bf16[16,64,128]{2,1,0:T(8,128)(2,1)S(1)} %all_to_all.32.near_ref, bf16[16,64,128]{2,1,0:T(8,128)(2,1)} %copy-done.1, ...), custom_call_target="tpu_custom_call" | custom-call | tf_op jit(solution)/shard_map/result/pallas_call | solution.py:263
  (7 shorter events, 0.3 us)
Async XLA Ops:
  7.2 114.9 %reduce-scatter.2.cloned.1.call-start = ((), (), s32[]{:S(2)}) async-start(), calls=%async_computation.7 | async-start | bytes 4456448 | tf_op jit(solution)/shard_map/grad/reduce_scatter | solution.py:320
  13.8 64.6 %copy-start = (bf16[1,384,4096]{2,1,0:T(8,128)(2,1)S(1)}, bf16[1,384,4096]{2,1,0:T(8,128)(2,1)}, u32[]{:S(2)}) copy-start(bf16[1,384,4096]{2,1,0:T(8,128)(2,1)} %param.4) | copy-start | bytes 9437188
  13.9 10.6 %collective-permute-start = (f32[16,64,128]{2,1,0:T(8,128)S(1)}, f32[16,64,128]{2,1,0:T(8,128)S(1)}, u32[]{:S(2)}, u32[]{:S(2)}) collective-permute-start(f32[16,64,128]{2,1,0:T(8,128)S(1)} %get-tuple-element.13), channel_id=1, source_target_pairs={{0,1},{1,0},{2,3},{3,2},{4,5},{5,4},{6,7},{7,6},{8,9},{9,8},{10,11... | collective-permute-start | bytes 1572872 | tf_op jit(solution)/shard_map/left_sum/ppermute | solution.py:313
  70.0 8.5 %collective-permute-start.1 = (bf16[16,64,128]{2,1,0:T(8,128)(2,1)S(1)}, bf16[16,64,128]{2,1,0:T(8,128)(2,1)S(1)}, u32[]{:S(2)}, u32[]{:S(2)}) collective-permute-start(bf16[16,64,128]{2,1,0:T(8,128)(2,1)S(1)} %all_to_all.32.near_ref), channel_id=1, source_target_pairs={{0,1},{1,0},{2,3},{3,2},{4,5},{5,4},{6,7},{7,6},{8,9},{9,8},{10,11... | collective-permute-start | bytes 786440 | tf_op jit(solution)/shard_map/left_gather/ppermute | solution.py:323
  78.4 2.9 %copy-start.1 = (bf16[16,64,128]{2,1,0:T(8,128)(2,1)}, bf16[16,64,128]{2,1,0:T(8,128)(2,1)S(1)}, u32[]{:S(2)}) copy-start(bf16[16,64,128]{2,1,0:T(8,128)(2,1)S(1)} %collective-permute-done.1.far_ref.far_hbm) | copy-start | bytes 786436
  109.1 13.0 %all-to-all-start.5 = ((bf16[16,16,128]{2,1,0:T(8,128)(2,1)}), bf16[16,16,128]{2,1,0:T(8,128)(2,1)S(1)}, u32[]{:S(2)}, u32[]{:S(2)}) async-start(bf16[16,16,128]{2,1,0:T(8,128)(2,1)} %broadcast_in_dim.13), calls=%async_computation.5 | async-start | bytes 131072 | tf_op jit(solution)/shard_map/right_sum/all_to_all | solution.py:331
Sparse Core Ops, SparseCore 0:
  38.0 76.2 reduce-scatter.1

commit v5 on v4

--- a/solution.py
+++ b/solution.py
@@ -230,9 +230,10 @@
     across = tiles_ref.shape[0] * high // RANK
     m_t = jnp.concatenate(
         [jnp.concatenate([tiles_ref[r * across + q] for q in range(across)], 1) for r in range(RANK // high)], 0
-    ).astype(F32)
+    )
     inv = inv_ref[...]
-    right_t = dot(inv, m_t, NN, precision=HI) / n_out
+    parts = dot(jnp.concatenate(terms(inv, 3), 0), m_t, NN)
+    right_t = (parts[:RANK] + parts[RANK : 2 * RANK] + parts[2 * RANK :]) / n_out
     q = dot(inv, right_t, TN, precision=HI)
     q_2 = terms(q, 2)
     copies[0].wait()
@@ -328,6 +329,7 @@
         mine = jnp.sum(got.astype(F32), 0).astype(BF16)
         got = lax.all_to_all(spread(mine, len(plane[0])), both_axes, 0, 0, axis_index_groups=plane)
         mine = jnp.sum(got.astype(F32), 0).astype(BF16)
+        inv, mine = lax.optimization_barrier((inv, mine))
         tiles = lax.all_to_all(spread(mine, len(column[0])), both_axes, 0, 0, axis_index_groups=column)
     update_t, new_carried = result(tiles, inv, near, far, grad_t, c, n_out)
     return (update_t.T, new_carried[None])

time: 132 us -> 132 us (level)
  waiting for transfers between devices: 5.7 us -> 8.7 us
  blocking collectives: 72.2 us -> 69.3 us
    all_to_all x1, waiting for transfers between devices: 3.02 us -> 6.02 us  [per_device(): lax.all_to_all(spread(mine, len(plane[0])), both_axes, 0, 0, axis_index_g...]
    all_to_all x1, blocking collectives: 15.1 us -> 12.2 us  [per_device(): lax.all_to_all(spread(mine, len(column[0])), both_axes, 0, 0, axis_index_...]
where the time goes in v5:
time: 132 us; the launch traced here: 131 us
  blocking collectives  69.3 us (52%)
  starting transfers between devices  20.9 us (16%)
  Pallas kernels  16.1 us (12%)
  between operations  14.8 us (11%)
  waiting for transfers between devices  8.7 us (7%)
    all_to_all x1, blocking collectives, per_device(): lax.all_to_all(spread(mine, len(second[0])), both_axes, 0, 0, axis_index_...  20.5 us
    all_to_all x1, blocking collectives, per_device(): got = lax.all_to_all(pair, both_axes, 0, 0, axis_index_groups=first)  13.2 us
    all_to_all x1, blocking collectives, per_device(): lax.all_to_all(spread(mine, len(column[0])), both_axes, 0, 0, axis_index_...  12.2 us
    all_to_all x1, blocking collectives, per_device(): got = lax.all_to_all(tiles, both_axes, 0, 0, axis_index_groups=column)  11.9 us
    all_to_all x1, blocking collectives, per_device(): lax.all_to_all(spread(mine, len(first[0])), both_axes, 0, 0, axis_index_g...  11.5 us
    ppermute x1, starting transfers between devices, per_device(): pair = (keep + lax.ppermute(give, 'outer', siblings)).astype(BF16)  9.06 us
    ppermute x1, starting transfers between devices, per_device(): far = lax.ppermute(near, 'outer', siblings)  7.32 us
    all_to_all x1, waiting for transfers between devices, per_device(): lax.all_to_all(spread(mine, len(plane[0])), both_axes, 0, 0, axis_index_g...  6.02 us
  transfers between devices with their start and end apart: 4, of which 3 were waited for; matrix products, arithmetic and copies ran while one was open for 1% of the time, Pallas kernels for 6%

profile of v5, /device:TPU:1, one launch (start us, length us, event | category | flops | bytes accessed | tf_op | source)
XLA Modules:
  0.0 130.8 jit_solution(3337522094182693546)
XLA Ops:
  7.2 0.0 reduce-scatter.2.cloned.1.call-start
  7.9 6.0 %first_part.1 = (f32[16,64,128]{2,1,0:T(8,128)S(1)}, f32[16,64,128]{2,1,0:T(8,128)S(1)}, bf16[16,512,256]{2,1,0:T(8,128)(2,1)}) custom-call(s32[1]{0:T(128)} %bitcast.7.seed_ref, bf16[384,512]{1,0:T(8,128)(2,1)} %bitcast.14, f32[256,512]{1,0:T(8,128)} %bitcast.10, bf16[384,4096]{1,0:T(8,128)(2,1)} %bitcast.8), custom_call_target="tpu_custom_call" | custom-call | tf_op jit(solution)/shard_map/first_part/pallas_call | solution.py:128
  13.8 0.0 copy-start
  13.9 9.1 %collective-permute-start = (f32[16,64,128]{2,1,0:T(8,128)S(1)}, f32[16,64,128]{2,1,0:T(8,128)S(1)}, u32[]{:S(2)}, u32[]{:S(2)}) collective-permute-start(f32[16,64,128]{2,1,0:T(8,128)S(1)} %get-tuple-element.15), channel_id=1, source_target_pairs={{0,1},{1,0},{2,3},{3,2},{4,5},{5,4},{6,7},{7,6},{8,9},{9,8},{10,11... | collective-permute-start | bytes 1572872 | tf_op jit(solution)/shard_map/left_sum/ppermute | solution.py:314
  22.9 1.5 %collective-permute-done = f32[16,64,128]{2,1,0:T(8,128)S(1)} collective-permute-done((f32[16,64,128]{2,1,0:T(8,128)S(1)}, f32[16,64,128]{2,1,0:T(8,128)S(1)}, u32[]{:S(2)}, u32[]{:S(2)}) %collective-permute-start) | collective-permute-done | bytes 524320 | tf_op jit(solution)/shard_map/left_sum/ppermute | solution.py:314
  24.4 0.1 add_convert_fusion
  24.5 13.2 %all_to_all.30 = bf16[16,64,128]{2,1,0:T(8,128)(2,1)S(1)} all-to-all(bf16[16,64,128]{2,1,0:T(8,128)(2,1)S(1)} %add_convert_fusion), channel_id=1, replica_groups={{0,32,64,96,128,160,192,224,256,288,320,352,384,416,448,480},{1,5,9,13,..., dimensions={0} | all-to-all | bytes 524288 | tf_op jit(solution)/shard_map/left_sum/all_to_all | solution.py:315
  37.8 0.0 reduce-scatter.2.cloned.1.call-update
  37.9 20.5 %all_to_all.31 = bf16[16,64,128]{2,1,0:T(8,128)(2,1)S(1)} all-to-all(bf16[16,64,128]{2,1,0:T(8,128)(2,1)S(1)} %broadcast_in_dim.10), channel_id=1, replica_groups={{0,2,4,6,8,10,12,14,16,18,20,22,24,26,28,30},{1,3,33,35,65,67,97,99,129..., dimensions={0} | all-to-all | bytes 524288 | tf_op jit(solution)/shard_map/left_sum/all_to_all | solution.py:318
  58.4 11.5 %all_to_all.32.near_ref = bf16[16,64,128]{2,1,0:T(8,128)(2,1)S(1)} all-to-all(bf16[16,64,128]{2,1,0:T(8,128)(2,1)S(1)} %broadcast_in_dim.11), channel_id=1, replica_groups={{0,32,64,96,128,160,192,224,256,288,320,352,384,416,448,480},{1,5,9,13,..., dimensions={0} | all-to-all | bytes 524288 | tf_op jit(solution)/shard_map/left_gather/all_to_all | solution.py:323
  70.0 7.3 %collective-permute-start.1 = (bf16[16,64,128]{2,1,0:T(8,128)(2,1)S(1)}, bf16[16,64,128]{2,1,0:T(8,128)(2,1)S(1)}, u32[]{:S(2)}, u32[]{:S(2)}) collective-permute-start(bf16[16,64,128]{2,1,0:T(8,128)(2,1)S(1)} %all_to_all.32.near_ref), channel_id=1, source_target_pairs={{0,1},{1,0},{2,3},{3,2},{4,5},{5,4},{6,7},{7,6},{8,9},{9,8},{10,11... | collective-permute-start | bytes 786440 | tf_op jit(solution)/shard_map/left_gather/ppermute | solution.py:324
  77.3 1.1 collective-permute-done.1.far_ref.far_hbm
  78.4 0.0 copy-done
  78.4 0.0 copy-start.1
  78.4 2.9 %right_part.1 = (bf16[16,16,128]{2,1,0:T(8,128)(2,1)S(1)}, f32[64,64]{1,0:T(8,128)S(1)}) custom-call(bf16[16,64,128]{2,1,0:T(8,128)(2,1)S(1)} %all_to_all.32.near_ref, bf16[16,64,128]{2,1,0:T(8,128)(2,1)S(1)} %collective-permute-done.1.far_ref.far_hbm, bf16[384,4096]{1,0:T(8,128)(2,1)S(1)} %bitcast.9, bf16[384,512]{1,0:T(8,128)(2,1)} %bitcast.15, ...), custom_call_target="tpu_custom_call" | custom-call | tf_op jit(solution)/shard_map/right_part/pallas_call | solution.py:215
  81.3 0.0 copy-done.1
  81.3 11.9 %all_to_all.33 = bf16[16,16,128]{2,1,0:T(8,128)(2,1)S(1)} all-to-all(bf16[16,16,128]{2,1,0:T(8,128)(2,1)S(1)} %get-tuple-element.18), channel_id=1, replica_groups={{0,1,4,5,8,9,12,13,16,17,20,21,24,25,28,29},{2,3,6,7,10,11,14,15,18,19,..., dimensions={0} | all-to-all | bytes 131072 | tf_op jit(solution)/shard_map/right_sum/all_to_all | solution.py:328
  93.2 0.7 broadcast_in_dim.12
  93.9 4.4 %all-to-all-start.4 = ((bf16[32,16,128]{2,1,0:T(8,128)(2,1)}), bf16[32,16,128]{2,1,0:T(8,128)(2,1)S(1)}, u32[]{:S(2)}, u32[]{:S(2)}) async-start(bf16[32,16,128]{2,1,0:T(8,128)(2,1)} %broadcast_in_dim.12), calls=%async_computation.4 | async-start | bytes 262144 | tf_op jit(solution)/shard_map/right_sum/all_to_all | solution.py:330
  98.4 4.8 %factor.1.inv_ref = f32[64,64]{1,0:T(8,128)S(1)} custom-call(f32[64,64]{1,0:T(8,128)S(1)} %get-tuple-element.17.gram_ref), custom_call_target="tpu_custom_call" | custom-call | flops 4000000 | bytes 2000000 | tf_op jit(solution)/shard_map/factor/pallas_call | solution.py:51
  103.2 6.0 %all-to-all-done.4 = bf16[32,16,128]{2,1,0:T(8,128)(2,1)S(1)} async-done(((bf16[32,16,128]{2,1,0:T(8,128)(2,1)}), bf16[32,16,128]{2,1,0:T(8,128)(2,1)S(1)}, u32[]{:S(2)}, u32[]{:S(2)}) %all-to-all-start.4) | async-done | bytes 131104 | tf_op jit(solution)/shard_map/right_sum/all_to_all | solution.py:330
  109.3 12.2 %all_to_all.34.tiles_ref = bf16[16,16,128]{2,1,0:T(8,128)(2,1)S(1)} all-to-all(bf16[16,16,128]{2,1,0:T(8,128)(2,1)S(1)} %broadcast_in_dim.13), channel_id=1, replica_groups={{0,1,4,5,8,9,12,13,16,17,20,21,24,25,28,29},{2,3,6,7,10,11,14,15,18,19,..., dimensions={0} | all-to-all | bytes 131072 | tf_op jit(solution)/shard_map/right_sum/all_to_all | solution.py:333
  121.5 0.0 reduce-scatter.2.cloned.1.call-done.grad_hbm
  121.5 2.4 %result.1 = (bf16[16,4096]{1,0:T(8,128)(2,1)}, f32[256,512]{1,0:T(8,128)}) custom-call(bf16[16,16,128]{2,1,0:T(8,128)(2,1)S(1)} %all_to_all.34.tiles_ref, f32[64,64]{1,0:T(8,128)S(1)} %factor.1.inv_ref, bf16[16,64,128]{2,1,0:T(8,128)(2,1)S(1)} %all_to_all.32.near_ref, bf16[16,64,128]{2,1,0:T(8,128)(2,1)} %copy-done.1, ...), custom_call_target="tpu_custom_call" | custom-call | tf_op jit(solution)/shard_map/result/pallas_call | solution.py:264
  (7 shorter events, 0.2 us)
Async XLA Ops:
  7.2 114.3 %reduce-scatter.2.cloned.1.call-start = ((), (), s32[]{:S(2)}) async-start(), calls=%async_computation.7 | async-start | bytes 4456448 | tf_op jit(solution)/shard_map/grad/reduce_scatter | solution.py:321
  13.8 64.6 %copy-start = (bf16[1,384,4096]{2,1,0:T(8,128)(2,1)S(1)}, bf16[1,384,4096]{2,1,0:T(8,128)(2,1)}, u32[]{:S(2)}) copy-start(bf16[1,384,4096]{2,1,0:T(8,128)(2,1)} %param.4) | copy-start | bytes 9437188
  13.9 10.6 %collective-permute-start = (f32[16,64,128]{2,1,0:T(8,128)S(1)}, f32[16,64,128]{2,1,0:T(8,128)S(1)}, u32[]{:S(2)}, u32[]{:S(2)}) collective-permute-start(f32[16,64,128]{2,1,0:T(8,128)S(1)} %get-tuple-element.15), channel_id=1, source_target_pairs={{0,1},{1,0},{2,3},{3,2},{4,5},{5,4},{6,7},{7,6},{8,9},{9,8},{10,11... | collective-permute-start | bytes 1572872 | tf_op jit(solution)/shard_map/left_sum/ppermute | solution.py:314
  70.0 8.5 %collective-permute-start.1 = (bf16[16,64,128]{2,1,0:T(8,128)(2,1)S(1)}, bf16[16,64,128]{2,1,0:T(8,128)(2,1)S(1)}, u32[]{:S(2)}, u32[]{:S(2)}) collective-permute-start(bf16[16,64,128]{2,1,0:T(8,128)(2,1)S(1)} %all_to_all.32.near_ref), channel_id=1, source_target_pairs={{0,1},{1,0},{2,3},{3,2},{4,5},{5,4},{6,7},{7,6},{8,9},{9,8},{10,11... | collective-permute-start | bytes 786440 | tf_op jit(solution)/shard_map/left_gather/ppermute | solution.py:324
  78.4 2.9 %copy-start.1 = (bf16[16,64,128]{2,1,0:T(8,128)(2,1)}, bf16[16,64,128]{2,1,0:T(8,128)(2,1)S(1)}, u32[]{:S(2)}) copy-start(bf16[16,64,128]{2,1,0:T(8,128)(2,1)S(1)} %collective-permute-done.1.far_ref.far_hbm) | copy-start | bytes 786436
  93.9 15.3 %all-to-all-start.4 = ((bf16[32,16,128]{2,1,0:T(8,128)(2,1)}), bf16[32,16,128]{2,1,0:T(8,128)(2,1)S(1)}, u32[]{:S(2)}, u32[]{:S(2)}) async-start(bf16[32,16,128]{2,1,0:T(8,128)(2,1)} %broadcast_in_dim.12), calls=%async_computation.4 | async-start | bytes 262144 | tf_op jit(solution)/shard_map/right_sum/all_to_all | solution.py:330
Sparse Core Ops, SparseCore 0:
  38.0 75.6 reduce-scatter.1
